TPU v7x, 128 devices: a whole 4x4x4 slice. The times are simulated.
128 devices in a mesh: grp: 8 (over y, core), blk: 16 (over x, z).
Axes of the slice: x: 4, y: 4, z: 4, core: 2. Of those that a mesh axis runs over, the one named last changes fastest.
Arguments:
- embeddings: float32 [32768, 768], P(('grp', 'blk')), may hold values from -6 to 6
- owner: int32 [32768, 1], P(('grp', 'blk')), may hold values from 0 to 7; in each aligned block of 256 rows (0 to 255, 256 to 511, ...) at most 128 rows name the same one
- cluster: int32 [32768], P(('grp', 'blk')), may hold values from 0 to 1
- order: int32 [32768], P(('grp', 'blk')), may hold values from 0 to 32767, each once
Outputs:
- nearest: float32 [32768], P(('grp', 'blk'))
Inputs may be any that keep to these rules, and one draw needn't show every extreme that they name: `owner`: in the rows of one device no group is named by more than 128 rows, a bound that some block reaches.
All inputs are finite; a program needn't handle non-finite values.
Results may differ from a plain program's by a relative error of at most 0.0013.
Values may be sent and summed in bfloat16 or wider, within the bound.
No kernel may reach another device: no remote copies, remote signals or barrier semaphores. Data moves between devices by JAX's collectives and lax.ppermute only.
A program may use at most 128 MiB of HBM per device.

v0:
```python
import jax
import jax.numpy as jnp
from jax import lax
from jax.sharding import PartitionSpec as P


def masked_best(queries, query_clus, query_order, keys, key_clus, key_order):
    scores = lax.dot_general(
        queries, keys, (((1,), (1,)), ((), ())), preferred_element_type=jnp.float32
    )
    forward = (query_clus[:, None] == key_clus[None, :]) & (key_clus[None, :] >= 0)
    earlier = forward & (key_order[None, :] < query_order[:, None])
    later = forward & (query_order[:, None] < key_order[None, :])
    low = jnp.float32(-1.0)
    rows_best = jnp.max(jnp.where(earlier, scores, low), axis=1)
    cols_best = jnp.max(jnp.where(later, scores, low), axis=0)
    return (rows_best, cols_best)


def local(embeddings, owner, cluster, order):
    groups = lax.axis_size("grp")
    row_count = embeddings.shape[0]
    width = embeddings.shape[1]
    capacity = max(2, 4 * row_count // groups)
    unit = (
        embeddings * lax.rsqrt(jnp.sum(embeddings * embeddings, axis=1, keepdims=True) + 1e-06)
    ).astype(jnp.bfloat16)
    target = owner[:, 0]
    onehot = (target[:, None] == jnp.arange(groups, dtype=jnp.int32)[None, :]).astype(jnp.int32)
    position = jnp.sum((jnp.cumsum(onehot, axis=0) - 1) * onehot, axis=1)
    flat = target * capacity + position
    slots = groups * capacity
    send_emb = (
        jnp.zeros((slots, width), jnp.bfloat16).at[flat].set(unit).reshape(groups, capacity, width)
    )
    send_clus = jnp.full((slots,), -1, jnp.int32).at[flat].set(cluster).reshape(groups, capacity)
    send_order = jnp.zeros((slots,), jnp.int32).at[flat].set(order).reshape(groups, capacity)
    got_emb, got_clus, got_order = (
        lax.all_to_all(send_emb, "grp", split_axis=0, concat_axis=0, tiled=True),
        lax.all_to_all(send_clus, "grp", split_axis=0, concat_axis=0, tiled=True),
        lax.all_to_all(send_order, "grp", split_axis=0, concat_axis=0, tiled=True),
    )
    keys = got_emb.reshape(slots, width)
    key_clus = got_clus.reshape(slots)
    key_order = got_order.reshape(slots)
    found, unused = masked_best(
        keys,
        key_clus,
        key_order,
        lax.all_gather(keys, "blk", axis=0, tiled=True),
        lax.all_gather(key_clus, "blk", axis=0, tiled=True),
        lax.all_gather(key_order, "blk", axis=0, tiled=True),
    )
    best = jnp.maximum(jnp.full((slots,), -1.0, jnp.float32), found)
    home = lax.all_to_all(
        best.reshape(groups, capacity), "grp", split_axis=0, concat_axis=0, tiled=True
    )
    return home.reshape(slots)[flat]


def solution(mesh):
    placed = (
        P(("grp", "blk"), None),
        P(("grp", "blk"), None),
        P(("grp", "blk")),
        P(("grp", "blk")),
    )
    return jax.shard_map(
        local, mesh=mesh, in_specs=placed, out_specs=P(("grp", "blk")), check_vma=False
    )
```

profile of v0, /device:TPU:1, one launch (start us, length us, event | category | flops | bytes accessed | tf_op | source)
XLA Modules:
  0.0 250.5 jit_solution(9749187350690088253)
XLA Ops:
  6.5 0.0 all-gather.2.cloned.1.call-start
  6.5 0.7 fusion.4
  7.2 0.6 reduce-window.6
  7.8 0.2 slice_reduce_fusion
  8.0 0.8 fusion.3
  8.8 0.7 compare_select_fusion
  9.5 1.3 multiply_reduce_fusion
  10.8 2.8 %scatter_custom_fusion.2 = bf16[1024,768]{1,0:T(8,128)(2,1)S(1)} fusion(s32[256]{0:T(256)S(1)} %bitcast.30, bf16[]{:T(256)} %constant.13.clone.1, f32[256,768]{1,0:T(8,128)} %param.4, f32[256]{0:T(256)S(1)} %add_rsqrt_fusion), kind=kCustom, calls=%fused_computation.7 | custom fusion | flops 393216 | bytes 2360322 | tf_op jit(solution)/shard_map/scatter | solution.py:34
  13.6 26.6 %all_to_all.29 = bf16[8,128,768]{2,1,0:T(8,128)(2,1)} all-to-all(bf16[8,128,768]{2,1,0:T(8,128)(2,1)S(1)} %bitcast.23), channel_id=1, replica_groups=mesh['grp'=8,'blk'=16] {'grp'}, dimensions={0} | all-to-all | bytes 3145728 | tf_op jit(solution)/shard_map/all_to_all | solution.py:39
  40.2 0.0 all-gather.2.cloned.1.call-update
  40.2 2.1 scatter_custom_fusion
  42.3 4.2 %all-to-all-start = ((s32[8,1,128]{2,1,0:T(1,128)}), s32[8,1,128]{2,1,0:T(1,128)S(1)}, u32[]{:S(2)}, u32[]{:S(2)}) async-start(s32[8,1,128]{2,1,0:T(1,128)} %bitcast.6), calls=%async_computation | async-start | bytes 8192 | tf_op jit(solution)/shard_map/all_to_all | solution.py:40
  46.5 2.1 scatter_custom_fusion.1
  48.6 2.5 all-to-all-done
  51.1 3.9 %all-to-all-start.1 = ((s32[8,1,128]{2,1,0:T(1,128)}), s32[8,1,128]{2,1,0:T(1,128)S(1)}, u32[]{:S(2)}, u32[]{:S(2)}) async-start(s32[8,1,128]{2,1,0:T(1,128)} %bitcast.8), calls=%async_computation.1 | async-start | bytes 8192 | tf_op jit(solution)/shard_map/all_to_all | solution.py:41
  55.0 21.8 %all_gather.9 = s32[16384]{0:T(1024)S(1)} all-gather(s32[1024]{0:T(1024)S(1)} %bitcast.24), channel_id=1, replica_groups=mesh['grp'=8,'blk'=16] {'blk'}, dimensions={0}, use_global_device_ids=true | all-gather | bytes 69632 | tf_op jit(solution)/shard_map/all_gather | solution.py:51
  76.7 0.0 all-to-all-done.1
  76.7 18.3 %all_gather.10 = s32[16384]{0:T(1024)S(1)} all-gather(s32[1024]{0:T(1024)S(1)} %bitcast.26), channel_id=1, replica_groups=mesh['grp'=8,'blk'=16] {'blk'}, dimensions={0}, use_global_device_ids=true | all-gather | bytes 69632 | tf_op jit(solution)/shard_map/all_gather | solution.py:52
  95.0 101.4 %all-gather.2.cloned.1.call-done = bf16[16384,768]{1,0:T(8,128)(2,1)} async-done(((bf16[1024,768]{1,0:T(8,128)(2,1)}), bf16[16384,768]{1,0:T(8,128)(2,1)}) %all-gather.2.cloned.1.call-update) | async-done | bytes 25165840 | tf_op jit(solution)/shard_map/all_gather | solution.py:50
  196.4 35.3 %select_reduce_fusion = f32[1024]{0:T(1024)S(1)} fusion(s32[16384]{0:T(1024)S(1)} %all_gather.10, s32[16384]{0:T(1024)S(1)} %all_gather.9, s32[1024]{0:T(1024)S(1)} %bitcast.27, s32[1024]{0:T(1024)S(1)} %bitcast.25, pred[16384]{0:T(1024)(128)(4,1)S(1)} %broadcast_compare_fusion, bf16[1024,768]{1,0:T(8,128)(2,1)} %bitcast.22, ...), kind=kOutput, calls=%fused_computation.4 | convolution fusion | flops 25870467072 | bytes 26898432 | tf_op jit(solution)/shard_map/dot_general | solution.py:8
  231.7 0.6 broadcast_maximum_fusion
  232.2 4.9 %all-to-all-start.3 = ((f32[8,1,128]{2,1,0:T(1,128)}), f32[8,1,128]{2,1,0:T(1,128)S(1)}, u32[]{:S(2)}, u32[]{:S(2)}) async-start(f32[8,1,128]{2,1,0:T(1,128)} %bitcast.12), calls=%async_computation.3 | async-start | bytes 8192 | tf_op jit(solution)/shard_map/all_to_all | solution.py:55
  237.1 4.6 %all-to-all-done.3 = f32[8,1,128]{2,1,0:T(1,128)S(1)} async-done(((f32[8,1,128]{2,1,0:T(1,128)}), f32[8,1,128]{2,1,0:T(1,128)S(1)}, u32[]{:S(2)}, u32[]{:S(2)}) %all-to-all-start.3) | async-done | bytes 4128 | tf_op jit(solution)/shard_map/all_to_all | solution.py:55
  241.7 1.9 gather_fusion
  (5 shorter events, 0.1 us)
Async XLA Ops:
  6.5 189.8 %all-gather.2.cloned.1.call-start = ((), (), s32[]{:S(2)}) async-start(), calls=%async_computation.4 | async-start | bytes 26738688 | tf_op jit(solution)/shard_map/all_gather | solution.py:50
  42.3 8.8 %all-to-all-start = ((s32[8,1,128]{2,1,0:T(1,128)}), s32[8,1,128]{2,1,0:T(1,128)S(1)}, u32[]{:S(2)}, u32[]{:S(2)}) async-start(s32[8,1,128]{2,1,0:T(1,128)} %bitcast.6), calls=%async_computation | async-start | bytes 8192 | tf_op jit(solution)/shard_map/all_to_all | solution.py:40
  51.1 25.6 %all-to-all-start.1 = ((s32[8,1,128]{2,1,0:T(1,128)}), s32[8,1,128]{2,1,0:T(1,128)S(1)}, u32[]{:S(2)}, u32[]{:S(2)}) async-start(s32[8,1,128]{2,1,0:T(1,128)} %bitcast.8), calls=%async_computation.1 | async-start | bytes 8192 | tf_op jit(solution)/shard_map/all_to_all | solution.py:41
  232.2 9.4 %all-to-all-start.3 = ((f32[8,1,128]{2,1,0:T(1,128)}), f32[8,1,128]{2,1,0:T(1,128)S(1)}, u32[]{:S(2)}, u32[]{:S(2)}) async-start(f32[8,1,128]{2,1,0:T(1,128)} %bitcast.12), calls=%async_computation.3 | async-start | bytes 8192 | tf_op jit(solution)/shard_map/all_to_all | solution.py:55
Sparse Core Ops, SparseCore 0:
  40.3 155.9 all-gather.1
where the time goes:
time: 251 us; the launch traced here: 250 us
  waiting for transfers between devices  108 us (43%)
  blocking collectives  66.7 us (27%)
  matrix products  35.3 us (14%)
  between operations  13.4 us (5%)
  starting transfers between devices  12.9 us (5%)
  other arithmetic  7.4 us (3%)
  local copies, waits for them, and re-layouts  6.39 us (3%)
    all_gather x1, waiting for transfers between devices, local(): lax.all_gather(keys, 'blk', axis=0, tiled=True)  101 us
    dot_general x1, matrix products, masked_best(): lax.dot_general(queries, keys, (((1,), (1,)), ((), ())), preferred_elemen...  35.3 us
    all_to_all x1, blocking collectives, local(): lax.all_to_all(send_emb, 'grp', split_axis=0, concat_axis=0, tiled=True)  26.6 us
    all_gather x1, blocking collectives, local(): lax.all_gather(key_clus, 'blk', axis=0, tiled=True)  21.8 us
    all_gather x1, blocking collectives, local(): lax.all_gather(key_order, 'blk', axis=0, tiled=True)  18.3 us
  transfers between devices with their start and end apart: 4, of which 3 were waited for; matrix products, arithmetic and copies ran while one was open for 2% of the time, Pallas kernels for 0%

commit v1 on v0

v1 whole, which is shorter than its diff:
```python
import functools

import jax
import jax.numpy as jnp
from jax import lax
from jax.experimental import pallas as pl
from jax.experimental.pallas import tpu as pltpu
from jax.sharding import PartitionSpec as P

GRID = 4
META = 16
SPAN = 32768.0

AXES = ("grp", "blk")


def device(x, y, z, core):
    return ((y % GRID) * 2 + core) * GRID * GRID + (x % GRID) * GRID + z % GRID


def permute(value, step):
    pairs = []
    for x in range(GRID):
        for y in range(GRID):
            for z in range(GRID):
                for core in range(2):
                    dx, dy, dz, dc = step(core)
                    pairs.append(
                        (device(x, y, z, core), device(x + dx, y + dy, z + dz, core ^ dc))
                    )
    return lax.ppermute(value, AXES, pairs)


def fetch(value, axis, sign):
    def step(core):
        offset = [0, 0, 0, 0]
        offset[axis] = -sign if core == 0 else sign
        return tuple(offset)

    return permute(value, step)


def jump(value, axis):
    def step(core):
        offset = [0, 0, 0, 0]
        offset[axis] = 2
        return tuple(offset)

    return permute(value, step)


def swap(value):
    return permute(value, lambda core: (0, 0, 0, 1))


def prepare_kernel(emb_ref, owner_ref, cluster_ref, order_ref, out_ref):
    rows, width = emb_ref.shape
    emb = emb_ref[...]
    scale = lax.rsqrt(jnp.sum(emb * emb, axis=1, keepdims=True) + 1e-06)
    out_ref[:rows, :] = (emb * scale).astype(jnp.bfloat16)
    order = order_ref[...]
    high = jnp.right_shift(order, 8)
    low = jnp.bitwise_and(order, 255)
    ident = owner_ref[...] * 2 + cluster_ref[...]
    line = lax.broadcasted_iota(jnp.int32, (META, rows), 0)
    meta = jnp.where(line == 0, high, jnp.where(line == 1, low, jnp.where(line == 2, ident, 0)))
    out_ref[rows:, :] = jnp.zeros((META, width), jnp.bfloat16)
    out_ref[rows:, :rows] = meta.astype(jnp.float32).astype(jnp.bfloat16)


def prepare(embeddings, owner, cluster, order):
    rows, width = embeddings.shape
    return pl.pallas_call(
        prepare_kernel,
        out_shape=jax.ShapeDtypeStruct((rows + META, width), jnp.bfloat16),
        compiler_params=pltpu.CompilerParams(vmem_limit_bytes=16 * 1024 * 1024),
    )(
        embeddings,
        owner.reshape(1, rows),
        cluster.reshape(1, rows),
        order.reshape(1, rows),
    )


def codes(meta):
    meta = meta.astype(jnp.float32)
    base = meta[2:3, :] * SPAN
    return base + meta[0:1, :] * 256.0 + meta[1:2, :], base


def score_kernel(counts, query_count, rows, last, *refs):
    query_refs = refs[: len(counts[0])]
    key_refs = refs[len(counts[0]) : len(counts[0]) + len(counts[1])]
    rest = refs[len(counts[0]) + len(counts[1]) :]
    place_ref, before_ref, out_ref, queries, keys, code, acc, query_sem, key_sem = rest
    block = rows + META
    copies = []
    for refs_, sizes, target, sem in (
        (query_refs, counts[0], queries, query_sem),
        (key_refs, counts[1], keys, key_sem),
    ):
        start = 0
        for index, (ref, size) in enumerate(zip(refs_, sizes)):
            copy = pltpu.make_async_copy(
                ref, target.at[pl.ds(start * block, size * block)], sem.at[index]
            )
            copy.start()
            copies.append(copy)
            start += size
    key_count = sum(counts[1])
    for copy in copies:
        copy.wait()
    acc[...] = before_ref[...]
    for index in range(query_count):
        line, _ = codes(queries[pl.ds(index * block + rows, META), :rows])
        code[index] = jnp.broadcast_to(line, (128, rows)).T

    def one_key(key_index, carry):
        key_at = pl.multiple_of(key_index * block, META)
        key = keys[pl.ds(key_at, rows), :]
        key_code, _ = codes(keys[pl.ds(key_at + rows, META), :rows])
        for index in range(query_count):
            query = queries[pl.ds(index * block, rows), :]
            scores = lax.dot_general(
                query, key, (((1,), (1,)), ((), ())), preferred_element_type=jnp.float32
            )
            query_code = code[index]
            query_base = jnp.floor(query_code * (1.0 / SPAN)) * SPAN
            best = acc[index]
            for lane in range(0, rows, 128):
                part = key_code[:, lane : lane + 128]
                allowed = (part < query_code) & (part >= query_base)
                best = jnp.maximum(best, jnp.where(allowed, scores[:, lane : lane + 128], -1.0))
            acc[index] = best
        return carry

    lax.fori_loop(0, key_count, one_key, 0)
    if last:
        for index in range(query_count):
            out_ref[place_ref[index]] = jnp.max(acc[index].T, axis=0, keepdims=True)
    else:
        out_ref[...] = acc[...]


def score(queries, keys, place, before, rows, last):
    width = queries[0].shape[1]
    block = rows + META
    sizes = [[v.shape[0] // block for v in group] for group in (queries, keys)]
    query_count, key_count = sum(sizes[0]), sum(sizes[1])
    if last:
        out = jax.ShapeDtypeStruct((query_count, 1, rows), jnp.float32)
    else:
        out = jax.ShapeDtypeStruct((query_count, rows, 128), jnp.float32)
    anywhere = pl.BlockSpec(memory_space=pl.ANY)
    vmem = pl.BlockSpec(memory_space=pltpu.VMEM)
    return pl.pallas_call(
        functools.partial(score_kernel, sizes, query_count, rows, last),
        out_shape=out,
        in_specs=[anywhere] * (len(queries) + len(keys))
        + [pl.BlockSpec(memory_space=pltpu.SMEM), vmem],
        out_specs=vmem,
        scratch_shapes=[
            pltpu.VMEM((query_count * block, width), jnp.bfloat16),
            pltpu.VMEM((key_count * block, width), jnp.bfloat16),
            pltpu.VMEM((query_count, rows, 128), jnp.float32),
            pltpu.VMEM((query_count, rows, 128), jnp.float32),
            pltpu.SemaphoreType.DMA((len(queries),)),
            pltpu.SemaphoreType.DMA((len(keys),)),
        ],
        compiler_params=pltpu.CompilerParams(vmem_limit_bytes=32 * 1024 * 1024),
        cost_estimate=pl.CostEstimate(
            flops=2 * query_count * key_count * rows * rows * width,
            bytes_accessed=(query_count + key_count) * block * width * 2,
            transcendentals=0,
        ),
    )(*queries, *keys, place, before)


def local(embeddings, owner, cluster, order):
    rows = embeddings.shape[0]
    block = rows + META
    own = prepare(embeddings, owner, cluster, order)
    pair = jnp.concatenate([own, swap(own)], axis=0)
    key_x = fetch(pair, 0, 1)
    key_z = fetch(pair, 2, 1)
    line_y = fetch(pair, 1, 1)
    far_y = jump(own, 1)
    key_xz = fetch(key_x, 2, -1)
    key_zz = fetch(key_z[:block], 2, 1)
    key_xx = fetch(jnp.concatenate([key_x[:block], key_z], axis=0), 0, 1)
    other_y = swap(jnp.concatenate([line_y, far_y], axis=0))
    key_xzz = fetch(key_xz, 2, -1)
    key_xxz = fetch(key_xz, 0, 1)
    key_far = jump(key_zz, 0)
    queries = [pair, line_y, far_y, other_y]
    index = lax.axis_index("grp")
    y, core = index // 2, index % 2
    side = 1 - 2 * core
    where_y = jnp.stack([y, y, y + side, y + side, y + 2, y - side, y - side, y + 2]) % GRID
    types = jnp.stack([core, 1 - core, core, 1 - core, core, 1 - core, core, 1 - core])
    place = (where_y * 2 + types).astype(jnp.int32)
    best = jnp.full((8, rows, 128), -1.0, jnp.float32)
    best = score(queries, [own, key_x, key_z], place, best, rows, False)
    best = score(queries, [key_xz, key_zz, key_xx], place, best, rows, False)
    best = score(queries, [key_xzz, key_xxz], place, best, rows, False)
    best = score(queries, [key_far], place, best, rows, True)
    home = lax.all_to_all(best, "grp", split_axis=0, concat_axis=0, tiled=True)
    return jnp.max(home.reshape(8, rows), axis=0)


def solution(mesh):
    placed = (
        P(("grp", "blk"), None),
        P(("grp", "blk"), None),
        P(("grp", "blk")),
        P(("grp", "blk")),
    )
    return jax.shard_map(
        local, mesh=mesh, in_specs=placed, out_specs=P(("grp", "blk")), check_vma=False
    )
```

time: 251 us -> 96.3 us (0.38)
  waiting for transfers between devices: 108 us -> 24.5 us
  blocking collectives: 66.7 us -> 9.34 us
  matrix products: 35.3 us -> 0 us
  Pallas kernels: 0 us -> 30.8 us
  between operations: 13.4 us -> 0.1 us
  starting transfers between devices: 12.9 us -> 23 us
  other arithmetic: 7.4 us -> 2.91 us
    all_gather x1 -> x0, waiting for transfers between devices: 101 us -> none  [local(): lax.all_gather(keys, 'blk', axis=0, tiled=True)]
    all_gather x2 -> x0, blocking collectives: 40 us -> none  [the longest x1 21.8 us: local(): lax.all_gather(key_clus, 'blk', axis=0, tiled=True)]
    dot_general x1 -> x0, matrix products: 35.3 us -> none  [masked_best(): lax.dot_general(queries, keys, (((1,), (1,)), ((), ())), preferred_elemen...]
    pallas_call x0 -> x5, Pallas kernels: none -> 30.8 us  [the longest x4 30.7 us: score(): pl.pallas_call(functools.partial(score_kernel, sizes, query_count, rows,...]
    ppermute x0 -> x12, waiting for transfers between devices: none -> 24.5 us  [permute(): return lax.ppermute(value, AXES, pairs)]
    ppermute x0 -> x12, starting transfers between devices: none -> 23 us  [permute(): return lax.ppermute(value, AXES, pairs)]
    all_to_all x1, blocking collectives: 26.6 us -> 9.34 us  [local(): home = lax.all_to_all(best, 'grp', split_axis=0, concat_axis=0, tiled=True)]
    all_to_all x3 -> x0, starting transfers between devices: 12.9 us -> none  [the longest x1 4.87 us: local(): lax.all_to_all(best.reshape(groups, capacity), 'grp', split_axis=0, conca...]
  transfers between devices with their start and end apart: 4 -> 12, of which waited for: 3 -> 3; matrix products, arithmetic and copies ran while one was open for 2% -> 5% of each run, Pallas kernels for 0% -> 28%
where the time goes in v1:
time: 96.3 us; the launch traced here: 95.9 us
  Pallas kernels  30.8 us (32%)
  waiting for transfers between devices  24.5 us (25%)
  starting transfers between devices  23 us (24%)
  blocking collectives  9.34 us (10%)
  local copies, waits for them, and re-layouts  5.24 us (5%)
  other arithmetic  2.91 us (3%)
    pallas_call x4, Pallas kernels, score(): pl.pallas_call(functools.partial(score_kernel, sizes, query_count, rows,...  30.7 us
    ppermute x12, waiting for transfers between devices, permute(): return lax.ppermute(value, AXES, pairs)  24.5 us
    ppermute x12, starting transfers between devices, permute(): return lax.ppermute(value, AXES, pairs)  23 us
    all_to_all x1, blocking collectives, local(): home = lax.all_to_all(best, 'grp', split_axis=0, concat_axis=0, tiled=True)  9.34 us
    unnamed x8, local copies, waits for them, and re-layouts  3.17 us
  transfers between devices with their start and end apart: 12, of which 3 were waited for; matrix products, arithmetic and copies ran while one was open for 5% of the time, Pallas kernels for 28%

profile of v1, /device:TPU:1, one launch (start us, length us, event | category | flops | bytes accessed | tf_op | source)
XLA Modules:
  0.0 95.9 jit_solution(16806488422573931817)
XLA Ops:
  0.0 1.1 %copy-done = f32[256,768]{1,0:T(8,128)S(1)} copy-done((f32[256,768]{1,0:T(8,128)S(1)}, f32[256,768]{1,0:T(8,128)}, u32[]{:S(2)}) %copy-start) | copy-done | bytes 786456
  1.1 0.7 copy-done.1
  1.8 0.7 copy-done.2
  2.5 0.7 copy-done.3
  3.2 0.1 shard_map.46.refs_4_
  3.3 1.5 %collective-permute-start = (bf16[272,768]{1,0:T(8,128)(2,1)S(1)}, bf16[272,768]{1,0:T(8,128)(2,1)S(1)}, u32[]{:S(2)}, u32[]{:S(2)}) collective-permute-start(bf16[272,768]{1,0:T(8,128)(2,1)S(1)} %shard_map.46.refs_4_), channel_id=1, source_target_pairs={{0,16},{16,0},{1,17},{17,1},{2,18},{18,2},{3,19},{19,3},{32,48},{4... | collective-permute-start | bytes 1253384 | tf_op jit(solution)/shard_map/ppermute | solution.py:31
  4.8 1.4 %collective-permute-done = bf16[272,768]{1,0:T(8,128)(2,1)S(1)} collective-permute-done((bf16[272,768]{1,0:T(8,128)(2,1)S(1)}, bf16[272,768]{1,0:T(8,128)(2,1)S(1)}, u32[]{:S(2)}, u32[]{:S(2)}) %collective-permute-start) | collective-permute-done | bytes 417824 | tf_op jit(solution)/shard_map/ppermute | solution.py:31
  6.3 1.4 %collective-permute-start.1 = (bf16[544,768]{1,0:T(8,128)(2,1)S(1)}, bf16[544,768]{1,0:T(8,128)(2,1)S(1)}, u32[]{:S(2)}, u32[]{:S(2)}) collective-permute-start(bf16[544,768]{1,0:T(8,128)(2,1)S(1)} %pad_maximum_fusion.2.refs_0_), channel_id=1, source_target_pairs={{0,96},{16,48},{1,97},{17,49},{2,98},{18,50},{3,99},{19,51},{32,0}... | collective-permute-start | bytes 2506760 | tf_op jit(solution)/shard_map/ppermute | solution.py:31
  7.7 1.2 %collective-permute-start.7 = (bf16[544,768]{1,0:T(8,128)(2,1)S(1)}, bf16[544,768]{1,0:T(8,128)(2,1)}, u32[]{:S(2)}, u32[]{:S(2)}) collective-permute-start(bf16[544,768]{1,0:T(8,128)(2,1)S(1)} %pad_maximum_fusion.2.refs_0_), channel_id=1, source_target_pairs={{0,12},{16,20},{1,13},{17,21},{2,14},{18,22},{3,15},{19,23},{32,44... | collective-permute-start | bytes 2506760 | tf_op jit(solution)/shard_map/ppermute | solution.py:31
  8.9 1.6 %collective-permute-start.4 = (bf16[544,768]{1,0:T(8,128)(2,1)S(1)}, bf16[544,768]{1,0:T(8,128)(2,1)S(1)}, u32[]{:S(2)}, u32[]{:S(2)}) collective-permute-start(bf16[544,768]{1,0:T(8,128)(2,1)S(1)} %pad_maximum_fusion.2.refs_0_), channel_id=1, source_target_pairs={{0,3},{16,17},{1,0},{17,18},{2,1},{18,19},{3,2},{19,16},{32,35},{4... | collective-permute-start | bytes 2506760 | tf_op jit(solution)/shard_map/ppermute | solution.py:31
  10.6 2.6 %collective-permute-start.2 = (bf16[272,768]{1,0:T(8,128)(2,1)S(1)}, bf16[272,768]{1,0:T(8,128)(2,1)S(1)}, u32[]{:S(2)}, u32[]{:S(2)}) collective-permute-start(bf16[272,768]{1,0:T(8,128)(2,1)S(1)} %shard_map.46.refs_4_), channel_id=1, source_target_pairs={{0,64},{16,80},{1,65},{17,81},{2,66},{18,82},{3,67},{19,83},{32,96... | collective-permute-start | bytes 1253384 | tf_op jit(solution)/shard_map/ppermute | solution.py:31
  13.2 15.5 %collective-permute-done.2.refs_2_ = bf16[272,768]{1,0:T(8,128)(2,1)S(1)} collective-permute-done((bf16[272,768]{1,0:T(8,128)(2,1)S(1)}, bf16[272,768]{1,0:T(8,128)(2,1)S(1)}, u32[]{:S(2)}, u32[]{:S(2)}) %collective-permute-start.2) | collective-permute-done | bytes 417824 | tf_op jit(solution)/shard_map/ppermute | solution.py:31
  28.7 1.1 %pad_maximum_fusion = bf16[816,768]{1,0:T(8,128)(2,1)} fusion(bf16[272,768]{1,0:T(8,128)(2,1)S(1)} %collective-permute-done.2.refs_2_, bf16[544,768]{1,0:T(8,128)(2,1)S(1)} %collective-permute-done.1.refs_1_), kind=kLoop, calls=%fused_computation | loop fusion | flops 2506752 | bytes 2506752 | tf_op jit(solution)/shard_map/concatenate | solution.py:191
  29.8 1.2 %collective-permute-start.3 = (bf16[816,768]{1,0:T(8,128)(2,1)}, bf16[816,768]{1,0:T(8,128)(2,1)}, u32[]{:S(2)}, u32[]{:S(2)}) collective-permute-start(bf16[816,768]{1,0:T(8,128)(2,1)} %pad_maximum_fusion), channel_id=1, source_target_pairs={{0,16},{16,0},{1,17},{17,1},{2,18},{18,2},{3,19},{19,3},{32,48},{4... | collective-permute-start | bytes 3760136 | tf_op jit(solution)/shard_map/ppermute | solution.py:31
  31.0 3.1 %collective-permute-start.8 = (bf16[544,768]{1,0:T(8,128)(2,1)}, bf16[544,768]{1,0:T(8,128)(2,1)}, u32[]{:S(2)}, u32[]{:S(2)}) collective-permute-start(bf16[544,768]{1,0:T(8,128)(2,1)} %collective-permute-done.7.refs_5_), channel_id=1, source_target_pairs={{0,1},{16,19},{1,2},{17,16},{2,3},{18,17},{3,0},{19,18},{32,33},{4... | collective-permute-start | bytes 2506760 | tf_op jit(solution)/shard_map/ppermute | solution.py:31
  34.1 1.1 %slice.9 = bf16[272,768]{1,0:T(8,128)(2,1)S(1)} slice(bf16[544,768]{1,0:T(8,128)(2,1)} %collective-permute-done.7.refs_5_), slice={[0:272], [0:768]} | slice | bytes 835584 | tf_op jit(solution)/shard_map/slice | solution.py:190
  35.2 1.1 %pad_maximum_fusion.1 = bf16[816,768]{1,0:T(8,128)(2,1)} fusion(bf16[544,768]{1,0:T(8,128)(2,1)S(1)} %collective-permute-done.4.refs_6_, bf16[272,768]{1,0:T(8,128)(2,1)S(1)} %slice.9), kind=kLoop, calls=%fused_computation.1 | loop fusion | flops 2506752 | bytes 2506752 | tf_op jit(solution)/shard_map/concatenate | solution.py:190
  36.3 1.2 %collective-permute-start.11 = (bf16[816,768]{1,0:T(8,128)(2,1)}, bf16[816,768]{1,0:T(8,128)(2,1)}, u32[]{:S(2)}, u32[]{:S(2)}) collective-permute-start(bf16[816,768]{1,0:T(8,128)(2,1)} %pad_maximum_fusion.1), channel_id=1, source_target_pairs={{0,12},{16,20},{1,13},{17,21},{2,14},{18,22},{3,15},{19,23},{32,44... | collective-permute-start | bytes 3760136 | tf_op jit(solution)/shard_map/ppermute | solution.py:31
  37.5 0.8 slice.8
  38.3 0.1 stack.41
  38.4 0.1 stack.38
  38.4 7.6 %collective-permute-done.8.refs_4_ = bf16[544,768]{1,0:T(8,128)(2,1)} collective-permute-done((bf16[544,768]{1,0:T(8,128)(2,1)}, bf16[544,768]{1,0:T(8,128)(2,1)}, u32[]{:S(2)}, u32[]{:S(2)}) %collective-permute-start.8) | collective-permute-done | bytes 835616 | tf_op jit(solution)/shard_map/ppermute | solution.py:31
  46.1 3.4 %collective-permute-start.10 = (bf16[544,768]{1,0:T(8,128)(2,1)}, bf16[544,768]{1,0:T(8,128)(2,1)S(1)}, u32[]{:S(2)}, u32[]{:S(2)}) collective-permute-start(bf16[544,768]{1,0:T(8,128)(2,1)} %collective-permute-done.8.refs_4_), channel_id=1, source_target_pairs={{0,12},{16,20},{1,13},{17,21},{2,14},{18,22},{3,15},{19,23},{32,44... | collective-permute-start | bytes 2506760 | tf_op jit(solution)/shard_map/ppermute | solution.py:31
  49.5 3.4 %collective-permute-start.9 = (bf16[544,768]{1,0:T(8,128)(2,1)}, bf16[544,768]{1,0:T(8,128)(2,1)S(1)}, u32[]{:S(2)}, u32[]{:S(2)}) collective-permute-start(bf16[544,768]{1,0:T(8,128)(2,1)} %collective-permute-done.8.refs_4_), channel_id=1, source_target_pairs={{0,1},{16,19},{1,2},{17,16},{2,3},{18,17},{3,0},{19,18},{32,33},{4... | collective-permute-start | bytes 2506760 | tf_op jit(solution)/shard_map/ppermute | solution.py:31
  52.9 2.2 %collective-permute-start.6 = (bf16[272,768]{1,0:T(8,128)(2,1)}, bf16[272,768]{1,0:T(8,128)(2,1)S(1)}, u32[]{:S(2)}, u32[]{:S(2)}) collective-permute-start(bf16[272,768]{1,0:T(8,128)(2,1)} %collective-permute-done.5.refs_5_), channel_id=1, source_target_pairs={{0,8},{16,24},{1,9},{17,25},{2,10},{18,26},{3,11},{19,27},{32,40},... | collective-permute-start | bytes 1253384 | tf_op jit(solution)/shard_map/ppermute | solution.py:31
  55.2 0.1 broadcast_in_dim.3.refs_8_
  55.2 9.0 %shard_map.47.refs_8_ = f32[8,256,128]{2,1,0:T(8,128)S(1)} custom-call(bf16[544,768]{1,0:T(8,128)(2,1)S(1)} %pad_maximum_fusion.2.refs_0_, bf16[544,768]{1,0:T(8,128)(2,1)S(1)} %collective-permute-done.1.refs_1_, bf16[272,768]{1,0:T(8,128)(2,1)S(1)} %collective-permute-done.2.refs_2_, bf16[816,768]{1,0:T(8,128)(2,1)} %collective-permute-done.3.refs_3_, ...), custom_call_target="tpu_custom_call" | custom-call | flops 4026531840 | bytes 5431296 | tf_op jit(solution)/shard_map/pallas_call | solution.py:156
  64.2 10.6 %shard_map.48.refs_7_ = f32[8,256,128]{2,1,0:T(8,128)S(1)} custom-call(bf16[544,768]{1,0:T(8,128)(2,1)S(1)} %pad_maximum_fusion.2.refs_0_, bf16[544,768]{1,0:T(8,128)(2,1)S(1)} %collective-permute-done.1.refs_1_, bf16[272,768]{1,0:T(8,128)(2,1)S(1)} %collective-permute-done.2.refs_2_, bf16[816,768]{1,0:T(8,128)(2,1)} %collective-permute-done.3.refs_3_, ...), custom_call_target="tpu_custom_call" | custom-call | flops 4831838208 | bytes 5849088 | tf_op jit(solution)/shard_map/pallas_call | solution.py:156
  74.9 7.5 %shard_map.49.refs_6_ = f32[8,256,128]{2,1,0:T(8,128)S(1)} custom-call(bf16[544,768]{1,0:T(8,128)(2,1)S(1)} %pad_maximum_fusion.2.refs_0_, bf16[544,768]{1,0:T(8,128)(2,1)S(1)} %collective-permute-done.1.refs_1_, bf16[272,768]{1,0:T(8,128)(2,1)S(1)} %collective-permute-done.2.refs_2_, bf16[816,768]{1,0:T(8,128)(2,1)} %collective-permute-done.3.refs_3_, ...), custom_call_target="tpu_custom_call" | custom-call | flops 3221225472 | bytes 5013504 | tf_op jit(solution)/shard_map/pallas_call | solution.py:156
  82.4 3.6 %shard_map.50 = f32[8,1,256]{2,1,0:T(1,128)S(1)} custom-call(bf16[544,768]{1,0:T(8,128)(2,1)S(1)} %pad_maximum_fusion.2.refs_0_, bf16[544,768]{1,0:T(8,128)(2,1)S(1)} %collective-permute-done.1.refs_1_, bf16[272,768]{1,0:T(8,128)(2,1)S(1)} %collective-permute-done.2.refs_2_, bf16[816,768]{1,0:T(8,128)(2,1)} %collective-permute-done.3.refs_3_, ...), custom_call_target="tpu_custom_call" | custom-call | flops 805306368 | bytes 3760128 | tf_op jit(solution)/shard_map/pallas_call | solution.py:156
  86.0 9.3 %all_to_all.5 = f32[8,1,256]{2,1,0:T(1,128)S(1)} all-to-all(f32[8,1,256]{2,1,0:T(1,128)S(1)} %shard_map.50), channel_id=1, replica_groups=mesh['grp'=8,'blk'=16] {'grp'}, dimensions={0} | all-to-all | bytes 16384 | tf_op jit(solution)/shard_map/all_to_all | solution.py:207
  95.3 0.6 reduce_max.9
  (16 shorter events, 0.1 us)
Async XLA Ops:
  0.0 1.1 %copy-start = (f32[256,768]{1,0:T(8,128)S(1)}, f32[256,768]{1,0:T(8,128)}, u32[]{:S(2)}) copy-start(f32[256,768]{1,0:T(8,128)} %emb_ref.1) | copy-start | bytes 2359300
  1.1 0.7 copy-start.1
  1.8 0.7 copy-start.2
  2.5 0.7 copy-start.3
  3.3 2.9 %collective-permute-start = (bf16[272,768]{1,0:T(8,128)(2,1)S(1)}, bf16[272,768]{1,0:T(8,128)(2,1)S(1)}, u32[]{:S(2)}, u32[]{:S(2)}) collective-permute-start(bf16[272,768]{1,0:T(8,128)(2,1)S(1)} %shard_map.46.refs_4_), channel_id=1, source_target_pairs={{0,16},{16,0},{1,17},{17,1},{2,18},{18,2},{3,19},{19,3},{32,48},{4... | collective-permute-start | bytes 1253384 | tf_op jit(solution)/shard_map/ppermute | solution.py:31
  6.3 22.4 %collective-permute-start.1 = (bf16[544,768]{1,0:T(8,128)(2,1)S(1)}, bf16[544,768]{1,0:T(8,128)(2,1)S(1)}, u32[]{:S(2)}, u32[]{:S(2)}) collective-permute-start(bf16[544,768]{1,0:T(8,128)(2,1)S(1)} %pad_maximum_fusion.2.refs_0_), channel_id=1, source_target_pairs={{0,96},{16,48},{1,97},{17,49},{2,98},{18,50},{3,99},{19,51},{32,0}... | collective-permute-start | bytes 2506760 | tf_op jit(solution)/shard_map/ppermute | solution.py:31
  7.7 23.3 %collective-permute-start.7 = (bf16[544,768]{1,0:T(8,128)(2,1)S(1)}, bf16[544,768]{1,0:T(8,128)(2,1)}, u32[]{:S(2)}, u32[]{:S(2)}) collective-permute-start(bf16[544,768]{1,0:T(8,128)(2,1)S(1)} %pad_maximum_fusion.2.refs_0_), channel_id=1, source_target_pairs={{0,12},{16,20},{1,13},{17,21},{2,14},{18,22},{3,15},{19,23},{32,44... | collective-permute-start | bytes 2506760 | tf_op jit(solution)/shard_map/ppermute | solution.py:31
  8.9 26.2 %collective-permute-start.4 = (bf16[544,768]{1,0:T(8,128)(2,1)S(1)}, bf16[544,768]{1,0:T(8,128)(2,1)S(1)}, u32[]{:S(2)}, u32[]{:S(2)}) collective-permute-start(bf16[544,768]{1,0:T(8,128)(2,1)S(1)} %pad_maximum_fusion.2.refs_0_), channel_id=1, source_target_pairs={{0,3},{16,17},{1,0},{17,18},{2,1},{18,19},{3,2},{19,16},{32,35},{4... | collective-permute-start | bytes 2506760 | tf_op jit(solution)/shard_map/ppermute | solution.py:31
  10.6 18.1 %collective-permute-start.2 = (bf16[272,768]{1,0:T(8,128)(2,1)S(1)}, bf16[272,768]{1,0:T(8,128)(2,1)S(1)}, u32[]{:S(2)}, u32[]{:S(2)}) collective-permute-start(bf16[272,768]{1,0:T(8,128)(2,1)S(1)} %shard_map.46.refs_4_), channel_id=1, source_target_pairs={{0,64},{16,80},{1,65},{17,81},{2,66},{18,82},{3,67},{19,83},{32,96... | collective-permute-start | bytes 1253384 | tf_op jit(solution)/shard_map/ppermute | solution.py:31
  29.8 25.3 %collective-permute-start.3 = (bf16[816,768]{1,0:T(8,128)(2,1)}, bf16[816,768]{1,0:T(8,128)(2,1)}, u32[]{:S(2)}, u32[]{:S(2)}) collective-permute-start(bf16[816,768]{1,0:T(8,128)(2,1)} %pad_maximum_fusion), channel_id=1, source_target_pairs={{0,16},{16,0},{1,17},{17,1},{2,18},{18,2},{3,19},{19,3},{32,48},{4... | collective-permute-start | bytes 3760136 | tf_op jit(solution)/shard_map/ppermute | solution.py:31
  31.0 15.0 %collective-permute-start.8 = (bf16[544,768]{1,0:T(8,128)(2,1)}, bf16[544,768]{1,0:T(8,128)(2,1)}, u32[]{:S(2)}, u32[]{:S(2)}) collective-permute-start(bf16[544,768]{1,0:T(8,128)(2,1)} %collective-permute-done.7.refs_5_), channel_id=1, source_target_pairs={{0,1},{16,19},{1,2},{17,16},{2,3},{18,17},{3,0},{19,18},{32,33},{4... | collective-permute-start | bytes 2506760 | tf_op jit(solution)/shard_map/ppermute | solution.py:31
  36.3 27.9 %collective-permute-start.11 = (bf16[816,768]{1,0:T(8,128)(2,1)}, bf16[816,768]{1,0:T(8,128)(2,1)}, u32[]{:S(2)}, u32[]{:S(2)}) collective-permute-start(bf16[816,768]{1,0:T(8,128)(2,1)} %pad_maximum_fusion.1), channel_id=1, source_target_pairs={{0,12},{16,20},{1,13},{17,21},{2,14},{18,22},{3,15},{19,23},{32,44... | collective-permute-start | bytes 3760136 | tf_op jit(solution)/shard_map/ppermute | solution.py:31
  38.3 14.6 %collective-permute-start.5 = (bf16[272,768]{1,0:T(8,128)(2,1)}, bf16[272,768]{1,0:T(8,128)(2,1)}, u32[]{:S(2)}, u32[]{:S(2)}) collective-permute-start(bf16[272,768]{1,0:T(8,128)(2,1)} %slice.8), channel_id=1, source_target_pairs={{0,3},{16,17},{1,0},{17,18},{2,1},{18,19},{3,2},{19,16},{32,35},{4... | collective-permute-start | bytes 1253384 | tf_op jit(solution)/shard_map/ppermute | solution.py:31
  46.1 28.8 %collective-permute-start.10 = (bf16[544,768]{1,0:T(8,128)(2,1)}, bf16[544,768]{1,0:T(8,128)(2,1)S(1)}, u32[]{:S(2)}, u32[]{:S(2)}) collective-permute-start(bf16[544,768]{1,0:T(8,128)(2,1)} %collective-permute-done.8.refs_4_), channel_id=1, source_target_pairs={{0,12},{16,20},{1,13},{17,21},{2,14},{18,22},{3,15},{19,23},{32,44... | collective-permute-start | bytes 2506760 | tf_op jit(solution)/shard_map/ppermute | solution.py:31
  49.5 25.3 %collective-permute-start.9 = (bf16[544,768]{1,0:T(8,128)(2,1)}, bf16[544,768]{1,0:T(8,128)(2,1)S(1)}, u32[]{:S(2)}, u32[]{:S(2)}) collective-permute-start(bf16[544,768]{1,0:T(8,128)(2,1)} %collective-permute-done.8.refs_4_), channel_id=1, source_target_pairs={{0,1},{16,19},{1,2},{17,16},{2,3},{18,17},{3,0},{19,18},{32,33},{4... | collective-permute-start | bytes 2506760 | tf_op jit(solution)/shard_map/ppermute | solution.py:31
  52.9 29.4 %collective-permute-start.6 = (bf16[272,768]{1,0:T(8,128)(2,1)}, bf16[272,768]{1,0:T(8,128)(2,1)S(1)}, u32[]{:S(2)}, u32[]{:S(2)}) collective-permute-start(bf16[272,768]{1,0:T(8,128)(2,1)} %collective-permute-done.5.refs_5_), channel_id=1, source_target_pairs={{0,8},{16,24},{1,9},{17,25},{2,10},{18,26},{3,11},{19,27},{32,40},... | collective-permute-start | bytes 1253384 | tf_op jit(solution)/shard_map/ppermute | solution.py:31

commit v2 on v1

v2 whole, which is shorter than its diff:
```python
import functools

import jax
import jax.numpy as jnp
from jax import lax
from jax.experimental import pallas as pl
from jax.experimental.pallas import tpu as pltpu
from jax.sharding import PartitionSpec as P

GRID = 4
META = 16
SPAN = 32768.0

AXES = ("grp", "blk")


def device(x, y, z, core):
    return ((y % GRID) * 2 + core) * GRID * GRID + (x % GRID) * GRID + z % GRID


def permute(value, step):
    pairs = []
    for x in range(GRID):
        for y in range(GRID):
            for z in range(GRID):
                for core in range(2):
                    dx, dy, dz, dc = step(core)
                    pairs.append(
                        (device(x, y, z, core), device(x + dx, y + dy, z + dz, core ^ dc))
                    )
    return lax.ppermute(value, AXES, pairs)


def fetch(value, axis, sign):
    def step(core):
        offset = [0, 0, 0, 0]
        offset[axis] = -sign if core == 0 else sign
        return tuple(offset)

    return permute(value, step)


def jump(value, axis):
    def step(core):
        offset = [0, 0, 0, 0]
        offset[axis] = 2
        return tuple(offset)

    return permute(value, step)


def swap(value):
    return permute(value, lambda core: (0, 0, 0, 1))


def prepare_kernel(emb_ref, numbers_ref, out_ref):
    rows, width = emb_ref.shape
    owner, cluster, order = numbers_ref[0:1, :], numbers_ref[1:2, :], numbers_ref[2:3, :]
    high = jnp.right_shift(order, 8)
    low = jnp.bitwise_and(order, 255)
    ident = owner * 2 + cluster
    line = lax.broadcasted_iota(jnp.int32, (META, rows), 0)
    meta = jnp.where(line == 0, high, jnp.where(line == 1, low, jnp.where(line == 2, ident, 0)))
    out_ref[rows:, :] = jnp.zeros((META, width), jnp.bfloat16)
    out_ref[rows:, :rows] = meta.astype(jnp.float32).astype(jnp.bfloat16)
    values = emb_ref[...]
    scale = lax.rsqrt(jnp.sum(values * values, axis=1, keepdims=True) + 1e-06)
    out_ref[:rows, :] = (values * scale).astype(jnp.bfloat16)


def prepare(embeddings, owner, cluster, order):
    rows, width = embeddings.shape
    vmem = pl.BlockSpec(memory_space=pltpu.VMEM)
    numbers = jnp.concatenate(
        [owner.reshape(1, rows), cluster.reshape(1, rows), order.reshape(1, rows)], axis=0
    )
    return pl.pallas_call(
        prepare_kernel,
        out_shape=jax.ShapeDtypeStruct((rows + META, width), jnp.bfloat16),
        in_specs=[vmem] * 2,
        out_specs=vmem,
        compiler_params=pltpu.CompilerParams(vmem_limit_bytes=16 * 1024 * 1024),
    )(embeddings, numbers)


def codes(meta):
    meta = meta.astype(jnp.float32)
    base = meta[2:3, :] * SPAN
    return base + meta[0:1, :] * 256.0 + meta[1:2, :], base


def score_kernel(tasks, sizes, columns_of, rows, last, *refs):
    block = rows + META
    refs = list(refs)
    arrays = [refs.pop(0) for _ in sizes]
    befores = [refs.pop(0) if more else None for _, _, more in tasks]
    place = refs.pop(0) if last else None
    columns = refs.pop()
    for name, slot in columns_of.items():
        for index in range(sizes[name]):
            line, _ = codes(arrays[name][index * block + rows : (index + 1) * block, :rows])
            columns[slot + index] = jnp.broadcast_to(line, (128, rows)).T
    done = 0
    for number, (queries, keys, _) in enumerate(tasks):
        places = [(name, index) for name in queries for index in range(sizes[name])]
        for query, (query_name, query_index) in enumerate(places):
            at = query_index * block
            code, base = codes(arrays[query_name][at + rows : at + block, :rows])
            before = befores[number]
            most = jnp.full((8, rows), -1.0, jnp.float32) if before is None else before[query]
            for name in keys:
                for index in range(sizes[name]):
                    scores = lax.dot_general(
                        arrays[name][index * block : index * block + rows, :],
                        arrays[query_name][at : at + rows, :],
                        (((1,), (1,)), ((), ())),
                        preferred_element_type=jnp.float32,
                    )
                    column = columns[columns_of[name] + index]
                    column = jnp.concatenate([column] * (rows // 128), axis=1)
                    allowed = (column < code) & (column >= base)
                    scores = jnp.where(allowed, scores, -1.0).reshape(rows // 8, 8, rows)
                    most = jnp.maximum(most, scores.max(axis=0))
            if last:
                refs[0][place[done]] = jnp.max(most, axis=0, keepdims=True)
            else:
                refs[number][query] = most
            done += 1


def score(tasks, rows, place=None):
    block = rows + META
    arrays = []

    def position(value):
        for index, other in enumerate(arrays):
            if other is value:
                return index
        arrays.append(value)
        return len(arrays) - 1

    plan = tuple(
        (tuple(map(position, queries)), tuple(map(position, keys)), before is not None)
        for queries, keys, before in tasks
    )
    width = arrays[0].shape[1]
    sizes = tuple(v.shape[0] // block for v in arrays)
    columns_of, count = {}, 0
    for _, keys, _ in plan:
        for name in keys:
            if name not in columns_of:
                columns_of[name] = count
                count += sizes[name]
    query_counts = [sum(sizes[n] for n in queries) for queries, _, _ in plan]
    pairs = sum(
        total * sum(sizes[n] for n in keys) for total, (_, keys, _) in zip(query_counts, plan)
    )
    befores = [before for _, _, before in tasks if before is not None]
    last = place is not None
    if last:
        out_shape = [jax.ShapeDtypeStruct((sum(query_counts), 1, rows), jnp.float32)]
    else:
        out_shape = [jax.ShapeDtypeStruct((total, 8, rows), jnp.float32) for total in query_counts]
    vmem = pl.BlockSpec(memory_space=pltpu.VMEM)
    return pl.pallas_call(
        functools.partial(score_kernel, plan, sizes, columns_of, rows, last),
        out_shape=out_shape,
        in_specs=[vmem] * (len(arrays) + len(befores))
        + [pl.BlockSpec(memory_space=pltpu.SMEM)] * last,
        out_specs=[vmem] * len(out_shape),
        scratch_shapes=[pltpu.VMEM((count, rows, 128), jnp.float32)],
        compiler_params=pltpu.CompilerParams(vmem_limit_bytes=8 * 1024 * 1024),
        cost_estimate=pl.CostEstimate(
            flops=2 * pairs * rows * width, bytes_accessed=10000, transcendentals=0
        ),
    )(*arrays, *befores, *([place] if last else []))


def local(embeddings, owner, cluster, order):
    rows = embeddings.shape[0]
    block = rows + META
    index = lax.axis_index("grp")
    y, core = index // 2, index % 2
    side = 1 - 2 * core
    steps = jnp.stack([y, y, y + side, y + side, y - side, y - side, y + 2, y + 2]) % GRID
    types = jnp.stack([core, 1 - core, core, 1 - core, 1 - core, core, core, 1 - core])
    place = (steps * 2 + types).astype(jnp.int32)
    own = prepare(embeddings, owner, cluster, order)
    pair = jnp.concatenate([own, swap(own)], axis=0)
    key_x = fetch(pair, 0, 1)
    key_z = fetch(pair, 2, 1)
    line_y = fetch(pair, 1, 1)
    line_2y = fetch(line_y, 1, 1)
    key_xz = fetch(key_x, 2, -1)
    key_zx = fetch(jnp.concatenate([key_x[:block], key_z], axis=0), 0, 1)
    key_2z = fetch(key_z[:block], 2, 1)
    other_y = swap(line_y)
    front, back = [pair, line_y], [other_y, line_2y]
    near = [own, key_x, key_z]
    (best_front,) = score([(front, near, None)], rows)
    key_xz, best_front = lax.optimization_barrier((key_xz, best_front))
    key_2x2z = jump(key_2z, 0)
    key_xzz = fetch(key_xz, 2, -1)
    key_xxz = fetch(key_xz, 0, 1)
    middle = [key_xz, key_zx, key_2z]
    best_front, best_back = score(
        [(front, middle, best_front), (back, near + middle, None)], rows
    )
    far = [key_xxz, key_xzz, key_2x2z]
    (best,) = score([(front, far, best_front), (back, far, best_back)], rows, place)
    home = lax.all_to_all(best, "grp", split_axis=0, concat_axis=0, tiled=True)
    return jnp.max(home.reshape(8, rows), axis=0)


def solution(mesh):
    placed = (
        P(("grp", "blk"), None),
        P(("grp", "blk"), None),
        P(("grp", "blk")),
        P(("grp", "blk")),
    )
    return jax.shard_map(
        local, mesh=mesh, in_specs=placed, out_specs=P(("grp", "blk")), check_vma=False
    )
```

time: 96.3 us -> 76.4 us (0.79)
  Pallas kernels: 30.8 us -> 18.4 us
  waiting for transfers between devices: 24.5 us -> 18 us
  blocking collectives: 9.34 us -> 11 us
  starting transfers between devices: 23 us -> 21.5 us
    pallas_call x4 -> x3, Pallas kernels: 30.7 us -> 18.2 us  [score(): pl.pallas_call(functools.partial(score_kernel, plan, sizes, columns_of, r...]
    ppermute x12, waiting for transfers between devices: 24.5 us -> 18 us  [permute(): return lax.ppermute(value, AXES, pairs)]
    slice x2, local copies, waits for them, and re-layouts: 1.83 us -> 0.06 us  [the longest x1 0.03 us: local(): key_2z = fetch(key_z[:block], 2, 1)]
    all_to_all x1, blocking collectives: 9.34 us -> 11 us  [local(): home = lax.all_to_all(best, 'grp', split_axis=0, concat_axis=0, tiled=True)]
    ppermute x12, starting transfers between devices: 23 us -> 21.5 us  [permute(): return lax.ppermute(value, AXES, pairs)]
    unnamed x8 -> x10, local copies, waits for them, and re-layouts: 3.17 us -> 4.33 us
  transfers between devices with their start and end apart: 12 -> 12, of which waited for: 3 -> 5; matrix products, arithmetic and copies ran while one was open for 5% -> 2% of each run, Pallas kernels for 28% -> 16%
where the time goes in v2:
time: 76.4 us; the launch traced here: 76 us
  starting transfers between devices  21.5 us (28%)
  Pallas kernels  18.4 us (24%)
  waiting for transfers between devices  18 us (24%)
  blocking collectives  11 us (14%)
  local copies, waits for them, and re-layouts  4.56 us (6%)
  other arithmetic  2.49 us (3%)
    ppermute x12, starting transfers between devices, permute(): return lax.ppermute(value, AXES, pairs)  21.5 us
    pallas_call x3, Pallas kernels, score(): pl.pallas_call(functools.partial(score_kernel, plan, sizes, columns_of, r...  18.2 us
    ppermute x12, waiting for transfers between devices, permute(): return lax.ppermute(value, AXES, pairs)  18 us
    all_to_all x1, blocking collectives, local(): home = lax.all_to_all(best, 'grp', split_axis=0, concat_axis=0, tiled=True)  11 us
    unnamed x10, local copies, waits for them, and re-layouts  4.33 us
  transfers between devices with their start and end apart: 12, of which 5 were waited for; matrix products, arithmetic and copies ran while one was open for 2% of the time, Pallas kernels for 16%

profile of v2, /device:TPU:1, one launch (start us, length us, event | category | flops | bytes accessed | tf_op | source)
XLA Modules:
  0.0 76.0 jit_solution(14857305053879640958)
XLA Ops:
  0.0 0.7 pad_add_fusion.numbers_ref
  0.7 1.1 %copy-done.4 = f32[256,768]{1,0:T(8,128)S(1)} copy-done((f32[256,768]{1,0:T(8,128)S(1)}, f32[256,768]{1,0:T(8,128)}, u32[]{:S(2)}) %copy-start.4) | copy-done | bytes 786456
  1.9 0.1 shard_map.46.refs_2_.refs_7_
  2.0 1.5 %collective-permute-start = (bf16[272,768]{1,0:T(8,128)(2,1)S(1)}, bf16[272,768]{1,0:T(8,128)(2,1)S(1)}, u32[]{:S(2)}, u32[]{:S(2)}) collective-permute-start(bf16[272,768]{1,0:T(8,128)(2,1)S(1)} %shard_map.46.refs_2_.refs_7_), channel_id=1, source_target_pairs={{0,16},{16,0},{1,17},{17,1},{2,18},{18,2},{3,19},{19,3},{32,48},{4... | collective-permute-start | bytes 1253384 | tf_op jit(solution)/shard_map/ppermute | solution.py:31
  3.5 1.4 %collective-permute-done = bf16[272,768]{1,0:T(8,128)(2,1)S(1)} collective-permute-done((bf16[272,768]{1,0:T(8,128)(2,1)S(1)}, bf16[272,768]{1,0:T(8,128)(2,1)S(1)}, u32[]{:S(2)}, u32[]{:S(2)}) %collective-permute-start) | collective-permute-done | bytes 417824 | tf_op jit(solution)/shard_map/ppermute | solution.py:31
  4.9 0.1 pad_maximum_fusion.1.refs_0_
  4.9 1.4 %collective-permute-start.2 = (bf16[544,768]{1,0:T(8,128)(2,1)S(1)}, bf16[544,768]{1,0:T(8,128)(2,1)S(1)}, u32[]{:S(2)}, u32[]{:S(2)}) collective-permute-start(bf16[544,768]{1,0:T(8,128)(2,1)S(1)} %pad_maximum_fusion.1.refs_0_), channel_id=1, source_target_pairs={{0,12},{16,20},{1,13},{17,21},{2,14},{18,22},{3,15},{19,23},{32,44... | collective-permute-start | bytes 2506760 | tf_op jit(solution)/shard_map/ppermute | solution.py:31
  6.3 1.6 %collective-permute-start.4 = (bf16[544,768]{1,0:T(8,128)(2,1)S(1)}, bf16[544,768]{1,0:T(8,128)(2,1)S(1)}, u32[]{:S(2)}, u32[]{:S(2)}) collective-permute-start(bf16[544,768]{1,0:T(8,128)(2,1)S(1)} %pad_maximum_fusion.1.refs_0_), channel_id=1, source_target_pairs={{0,3},{16,17},{1,0},{17,18},{2,1},{18,19},{3,2},{19,16},{32,35},{4... | collective-permute-start | bytes 2506760 | tf_op jit(solution)/shard_map/ppermute | solution.py:31
  7.9 1.3 %collective-permute-start.1 = (bf16[544,768]{1,0:T(8,128)(2,1)S(1)}, bf16[544,768]{1,0:T(8,128)(2,1)S(1)}, u32[]{:S(2)}, u32[]{:S(2)}) collective-permute-start(bf16[544,768]{1,0:T(8,128)(2,1)S(1)} %pad_maximum_fusion.1.refs_0_), channel_id=1, source_target_pairs={{0,96},{16,48},{1,97},{17,49},{2,98},{18,50},{3,99},{19,51},{32,0}... | collective-permute-start | bytes 2506760 | tf_op jit(solution)/shard_map/ppermute | solution.py:31
  9.2 8.3 %collective-permute-done.2.refs_3_.refs_8_ = bf16[544,768]{1,0:T(8,128)(2,1)S(1)} collective-permute-done((bf16[544,768]{1,0:T(8,128)(2,1)S(1)}, bf16[544,768]{1,0:T(8,128)(2,1)S(1)}, u32[]{:S(2)}, u32[]{:S(2)}) %collective-permute-start.2) | collective-permute-done | bytes 835616 | tf_op jit(solution)/shard_map/ppermute | solution.py:31
  17.6 4.1 %collective-permute-start.3 = (bf16[544,768]{1,0:T(8,128)(2,1)S(1)}, bf16[544,768]{1,0:T(8,128)(2,1)}, u32[]{:S(2)}, u32[]{:S(2)}) collective-permute-start(bf16[544,768]{1,0:T(8,128)(2,1)S(1)} %collective-permute-done.2.refs_3_.refs_8_), channel_id=1, source_target_pairs={{0,1},{16,19},{1,2},{17,16},{2,3},{18,17},{3,0},{19,18},{32,33},{4... | collective-permute-start | bytes 2506760 | tf_op jit(solution)/shard_map/ppermute | solution.py:31
  21.8 0.0 collective-permute-done.4.refs_4_.refs_9_
  21.8 1.1 %pad_maximum_fusion = bf16[816,768]{1,0:T(8,128)(2,1)} fusion(bf16[544,768]{1,0:T(8,128)(2,1)S(1)} %collective-permute-done.4.refs_4_.refs_9_, bf16[272,768]{1,0:T(8,128)(2,1)S(1)} %slice.9), kind=kLoop, calls=%fused_computation | loop fusion | flops 2506752 | bytes 2506752 | tf_op jit(solution)/shard_map/concatenate | solution.py:195
  22.9 1.3 %collective-permute-start.10 = (bf16[544,768]{1,0:T(8,128)(2,1)S(1)}, bf16[544,768]{1,0:T(8,128)(2,1)S(1)}, u32[]{:S(2)}, u32[]{:S(2)}) collective-permute-start(bf16[544,768]{1,0:T(8,128)(2,1)S(1)} %collective-permute-done.1.refs_1_), channel_id=1, source_target_pairs={{0,96},{16,48},{1,97},{17,49},{2,98},{18,50},{3,99},{19,51},{32,0}... | collective-permute-start | bytes 2506760 | tf_op jit(solution)/shard_map/ppermute | solution.py:31
  24.2 0.1 collective-permute-start.7
  24.3 6.7 %collective-permute-start.9 = (bf16[544,768]{1,0:T(8,128)(2,1)S(1)}, bf16[544,768]{1,0:T(8,128)(2,1)}, u32[]{:S(2)}, u32[]{:S(2)}) collective-permute-start(bf16[544,768]{1,0:T(8,128)(2,1)S(1)} %collective-permute-done.1.refs_1_), channel_id=1, source_target_pairs={{0,16},{16,0},{1,17},{17,1},{2,18},{18,2},{3,19},{19,3},{32,48},{4... | collective-permute-start | bytes 2506760 | tf_op jit(solution)/shard_map/ppermute | solution.py:31
  31.1 2.4 %shard_map.47.refs_10_ = f32[4,8,256]{2,1,0:T(8,128)S(1)} custom-call(bf16[544,768]{1,0:T(8,128)(2,1)S(1)} %pad_maximum_fusion.1.refs_0_, bf16[544,768]{1,0:T(8,128)(2,1)S(1)} %collective-permute-done.1.refs_1_, bf16[272,768]{1,0:T(8,128)(2,1)S(1)} %shard_map.46.refs_2_.refs_7_, bf16[544,768]{1,0:T(8,128)(2,1)S(1)} %collective-permute-done.2.refs_3_.refs_8_, ...), custom_call_target="tpu_custom_call" | custom-call | flops 7864320 | bytes 10000 | tf_op jit(solution)/shard_map/pallas_call | solution.py:165
  33.5 1.0 %collective-permute-start.5 = (bf16[544,768]{1,0:T(8,128)(2,1)}, bf16[544,768]{1,0:T(8,128)(2,1)}, u32[]{:S(2)}, u32[]{:S(2)}) collective-permute-start(bf16[544,768]{1,0:T(8,128)(2,1)} %collective-permute-done.3.refs_2_), channel_id=1, source_target_pairs={{0,12},{16,20},{1,13},{17,21},{2,14},{18,22},{3,15},{19,23},{32,44... | collective-permute-start | bytes 2506760 | tf_op jit(solution)/shard_map/ppermute | solution.py:31
  34.5 2.2 %collective-permute-done.7.refs_4_ = bf16[272,768]{1,0:T(8,128)(2,1)} collective-permute-done((bf16[272,768]{1,0:T(8,128)(2,1)S(1)}, bf16[272,768]{1,0:T(8,128)(2,1)}, u32[]{:S(2)}, u32[]{:S(2)}) %collective-permute-start.7) | collective-permute-done | bytes 417824 | tf_op jit(solution)/shard_map/ppermute | solution.py:31
  36.7 0.6 collective-permute-start.6
  37.3 0.9 %copy-done.2 = bf16[544,768]{1,0:T(8,128)(2,1)} copy-done((bf16[544,768]{1,0:T(8,128)(2,1)}, bf16[544,768]{1,0:T(8,128)(2,1)S(1)}, u32[]{:S(2)}) %copy-start.2) | copy-done | bytes 835608
  38.2 1.9 %collective-permute-start.8 = (bf16[272,768]{1,0:T(8,128)(2,1)}, bf16[272,768]{1,0:T(8,128)(2,1)S(1)}, u32[]{:S(2)}, u32[]{:S(2)}) collective-permute-start(bf16[272,768]{1,0:T(8,128)(2,1)} %collective-permute-done.7.refs_4_), channel_id=1, source_target_pairs={{0,8},{16,24},{1,9},{17,25},{2,10},{18,26},{3,11},{19,27},{32,40},... | collective-permute-start | bytes 1253384 | tf_op jit(solution)/shard_map/ppermute | solution.py:31
  40.1 0.1 stack.41
  40.2 0.1 stack.38
  40.3 1.1 %copy-done.1 = bf16[544,768]{1,0:T(8,128)(2,1)S(1)} copy-done((bf16[544,768]{1,0:T(8,128)(2,1)S(1)}, bf16[544,768]{1,0:T(8,128)(2,1)}, u32[]{:S(2)}) %copy-start.1) | copy-done | bytes 835608
  41.4 1.1 %copy-done.3 = bf16[544,768]{1,0:T(8,128)(2,1)S(1)} copy-done((bf16[544,768]{1,0:T(8,128)(2,1)S(1)}, bf16[544,768]{1,0:T(8,128)(2,1)}, u32[]{:S(2)}) %copy-start.3) | copy-done | bytes 835608
  42.6 9.6 %shard_map.48 = (f32[4,8,256]{2,1,0:T(8,128)S(1)}, f32[4,8,256]{2,1,0:T(8,128)S(1)}) custom-call(bf16[544,768]{1,0:T(8,128)(2,1)S(1)} %pad_maximum_fusion.1.refs_0_, bf16[544,768]{1,0:T(8,128)(2,1)S(1)} %collective-permute-done.1.refs_1_, bf16[544,768]{1,0:T(8,128)(2,1)} %collective-permute-done.3.refs_2_, bf16[816,768]{1,0:T(8,128)(2,1)} %collective-permute-done.11.refs_3_, ...), custom_call_target="tpu_custom_call" | custom-call | flops 26738688 | bytes 10000 | tf_op jit(solution)/shard_map/pallas_call | solution.py:165
  52.1 5.8 %collective-permute-done.8.refs_4_ = bf16[272,768]{1,0:T(8,128)(2,1)S(1)} collective-permute-done((bf16[272,768]{1,0:T(8,128)(2,1)}, bf16[272,768]{1,0:T(8,128)(2,1)S(1)}, u32[]{:S(2)}, u32[]{:S(2)}) %collective-permute-start.8) | collective-permute-done | bytes 417824 | tf_op jit(solution)/shard_map/ppermute | solution.py:31
  57.9 0.2 collective-permute-done.5.refs_2_
  58.2 6.3 %shard_map.49 = f32[8,1,256]{2,1,0:T(1,128)S(1)} custom-call(bf16[544,768]{1,0:T(8,128)(2,1)S(1)} %pad_maximum_fusion.1.refs_0_, bf16[544,768]{1,0:T(8,128)(2,1)S(1)} %collective-permute-done.1.refs_1_, bf16[544,768]{1,0:T(8,128)(2,1)} %collective-permute-done.5.refs_2_, bf16[544,768]{1,0:T(8,128)(2,1)} %collective-permute-done.6.refs_3_, ...), custom_call_target="tpu_custom_call" | custom-call | flops 15728640 | bytes 10000 | tf_op jit(solution)/shard_map/pallas_call | solution.py:165
  64.4 11.0 %all_to_all.5 = f32[8,1,256]{2,1,0:T(1,128)S(1)} all-to-all(f32[8,1,256]{2,1,0:T(1,128)S(1)} %shard_map.49), channel_id=1, replica_groups=mesh['grp'=8,'blk'=16] {'grp'}, dimensions={0} | all-to-all | bytes 16384 | tf_op jit(solution)/shard_map/all_to_all | solution.py:211
  75.4 0.6 reduce_max.9
  (16 shorter events, 0.1 us)
Async XLA Ops:
  0.7 1.1 %copy-start.4 = (f32[256,768]{1,0:T(8,128)S(1)}, f32[256,768]{1,0:T(8,128)}, u32[]{:S(2)}) copy-start(f32[256,768]{1,0:T(8,128)} %emb_ref.1) | copy-start | bytes 2359300
  2.0 2.9 %collective-permute-start = (bf16[272,768]{1,0:T(8,128)(2,1)S(1)}, bf16[272,768]{1,0:T(8,128)(2,1)S(1)}, u32[]{:S(2)}, u32[]{:S(2)}) collective-permute-start(bf16[272,768]{1,0:T(8,128)(2,1)S(1)} %shard_map.46.refs_2_.refs_7_), channel_id=1, source_target_pairs={{0,16},{16,0},{1,17},{17,1},{2,18},{18,2},{3,19},{19,3},{32,48},{4... | collective-permute-start | bytes 1253384 | tf_op jit(solution)/shard_map/ppermute | solution.py:31
  4.9 12.6 %collective-permute-start.2 = (bf16[544,768]{1,0:T(8,128)(2,1)S(1)}, bf16[544,768]{1,0:T(8,128)(2,1)S(1)}, u32[]{:S(2)}, u32[]{:S(2)}) collective-permute-start(bf16[544,768]{1,0:T(8,128)(2,1)S(1)} %pad_maximum_fusion.1.refs_0_), channel_id=1, source_target_pairs={{0,12},{16,20},{1,13},{17,21},{2,14},{18,22},{3,15},{19,23},{32,44... | collective-permute-start | bytes 2506760 | tf_op jit(solution)/shard_map/ppermute | solution.py:31
  6.3 15.5 %collective-permute-start.4 = (bf16[544,768]{1,0:T(8,128)(2,1)S(1)}, bf16[544,768]{1,0:T(8,128)(2,1)S(1)}, u32[]{:S(2)}, u32[]{:S(2)}) collective-permute-start(bf16[544,768]{1,0:T(8,128)(2,1)S(1)} %pad_maximum_fusion.1.refs_0_), channel_id=1, source_target_pairs={{0,3},{16,17},{1,0},{17,18},{2,1},{18,19},{3,2},{19,16},{32,35},{4... | collective-permute-start | bytes 2506760 | tf_op jit(solution)/shard_map/ppermute | solution.py:31
  7.9 14.9 %collective-permute-start.1 = (bf16[544,768]{1,0:T(8,128)(2,1)S(1)}, bf16[544,768]{1,0:T(8,128)(2,1)S(1)}, u32[]{:S(2)}, u32[]{:S(2)}) collective-permute-start(bf16[544,768]{1,0:T(8,128)(2,1)S(1)} %pad_maximum_fusion.1.refs_0_), channel_id=1, source_target_pairs={{0,96},{16,48},{1,97},{17,49},{2,98},{18,50},{3,99},{19,51},{32,0}... | collective-permute-start | bytes 2506760 | tf_op jit(solution)/shard_map/ppermute | solution.py:31
  17.6 13.5 %copy-start = (bf16[544,768]{1,0:T(8,128)(2,1)}, bf16[544,768]{1,0:T(8,128)(2,1)S(1)}, u32[]{:S(2)}) copy-start(bf16[544,768]{1,0:T(8,128)(2,1)S(1)} %collective-permute-done.2.refs_3_.refs_8_) | copy-start | bytes 2506756
  17.6 15.9 %collective-permute-start.3 = (bf16[544,768]{1,0:T(8,128)(2,1)S(1)}, bf16[544,768]{1,0:T(8,128)(2,1)}, u32[]{:S(2)}, u32[]{:S(2)}) collective-permute-start(bf16[544,768]{1,0:T(8,128)(2,1)S(1)} %collective-permute-done.2.refs_3_.refs_8_), channel_id=1, source_target_pairs={{0,1},{16,19},{1,2},{17,16},{2,3},{18,17},{3,0},{19,18},{32,33},{4... | collective-permute-start | bytes 2506760 | tf_op jit(solution)/shard_map/ppermute | solution.py:31
  22.9 17.4 %collective-permute-start.11 = (bf16[816,768]{1,0:T(8,128)(2,1)}, bf16[816,768]{1,0:T(8,128)(2,1)}, u32[]{:S(2)}, u32[]{:S(2)}) collective-permute-start(bf16[816,768]{1,0:T(8,128)(2,1)} %pad_maximum_fusion), channel_id=1, source_target_pairs={{0,12},{16,20},{1,13},{17,21},{2,14},{18,22},{3,15},{19,23},{32,44... | collective-permute-start | bytes 3760136 | tf_op jit(solution)/shard_map/ppermute | solution.py:31
  22.9 14.4 %collective-permute-start.10 = (bf16[544,768]{1,0:T(8,128)(2,1)S(1)}, bf16[544,768]{1,0:T(8,128)(2,1)S(1)}, u32[]{:S(2)}, u32[]{:S(2)}) collective-permute-start(bf16[544,768]{1,0:T(8,128)(2,1)S(1)} %collective-permute-done.1.refs_1_), channel_id=1, source_target_pairs={{0,96},{16,48},{1,97},{17,49},{2,98},{18,50},{3,99},{19,51},{32,0}... | collective-permute-start | bytes 2506760 | tf_op jit(solution)/shard_map/ppermute | solution.py:31
  24.2 12.5 %collective-permute-start.7 = (bf16[272,768]{1,0:T(8,128)(2,1)S(1)}, bf16[272,768]{1,0:T(8,128)(2,1)}, u32[]{:S(2)}, u32[]{:S(2)}) collective-permute-start(bf16[272,768]{1,0:T(8,128)(2,1)S(1)} %slice.8), channel_id=1, source_target_pairs={{0,3},{16,17},{1,0},{17,18},{2,1},{18,19},{3,2},{19,16},{32,35},{4... | collective-permute-start | bytes 1253384 | tf_op jit(solution)/shard_map/ppermute | solution.py:31
  24.3 16.0 %collective-permute-start.9 = (bf16[544,768]{1,0:T(8,128)(2,1)S(1)}, bf16[544,768]{1,0:T(8,128)(2,1)}, u32[]{:S(2)}, u32[]{:S(2)}) collective-permute-start(bf16[544,768]{1,0:T(8,128)(2,1)S(1)} %collective-permute-done.1.refs_1_), channel_id=1, source_target_pairs={{0,16},{16,0},{1,17},{17,1},{2,18},{18,2},{3,19},{19,3},{32,48},{4... | collective-permute-start | bytes 2506760 | tf_op jit(solution)/shard_map/ppermute | solution.py:31
  33.5 24.7 %collective-permute-start.5 = (bf16[544,768]{1,0:T(8,128)(2,1)}, bf16[544,768]{1,0:T(8,128)(2,1)}, u32[]{:S(2)}, u32[]{:S(2)}) collective-permute-start(bf16[544,768]{1,0:T(8,128)(2,1)} %collective-permute-done.3.refs_2_), channel_id=1, source_target_pairs={{0,12},{16,20},{1,13},{17,21},{2,14},{18,22},{3,15},{19,23},{32,44... | collective-permute-start | bytes 2506760 | tf_op jit(solution)/shard_map/ppermute | solution.py:31
  36.7 21.5 %collective-permute-start.6 = (bf16[544,768]{1,0:T(8,128)(2,1)}, bf16[544,768]{1,0:T(8,128)(2,1)}, u32[]{:S(2)}, u32[]{:S(2)}) collective-permute-start(bf16[544,768]{1,0:T(8,128)(2,1)} %collective-permute-done.3.refs_2_), channel_id=1, source_target_pairs={{0,1},{16,19},{1,2},{17,16},{2,3},{18,17},{3,0},{19,18},{32,33},{4... | collective-permute-start | bytes 2506760 | tf_op jit(solution)/shard_map/ppermute | solution.py:31
  37.3 0.9 %copy-start.2 = (bf16[544,768]{1,0:T(8,128)(2,1)}, bf16[544,768]{1,0:T(8,128)(2,1)S(1)}, u32[]{:S(2)}) copy-start(bf16[544,768]{1,0:T(8,128)(2,1)S(1)} %collective-permute-done.10.refs_6_) | copy-start | bytes 2506756
  38.2 19.7 %collective-permute-start.8 = (bf16[272,768]{1,0:T(8,128)(2,1)}, bf16[272,768]{1,0:T(8,128)(2,1)S(1)}, u32[]{:S(2)}, u32[]{:S(2)}) collective-permute-start(bf16[272,768]{1,0:T(8,128)(2,1)} %collective-permute-done.7.refs_4_), channel_id=1, source_target_pairs={{0,8},{16,24},{1,9},{17,25},{2,10},{18,26},{3,11},{19,27},{32,40},... | collective-permute-start | bytes 1253384 | tf_op jit(solution)/shard_map/ppermute | solution.py:31
  40.3 1.2 %copy-start.1 = (bf16[544,768]{1,0:T(8,128)(2,1)S(1)}, bf16[544,768]{1,0:T(8,128)(2,1)}, u32[]{:S(2)}) copy-start(bf16[544,768]{1,0:T(8,128)(2,1)} %copy-done) | copy-start | bytes 2506756
  41.4 1.1 %copy-start.3 = (bf16[544,768]{1,0:T(8,128)(2,1)S(1)}, bf16[544,768]{1,0:T(8,128)(2,1)}, u32[]{:S(2)}) copy-start(bf16[544,768]{1,0:T(8,128)(2,1)} %copy-done.2) | copy-start | bytes 2506756

commit v3 on v2

--- a/solution.py
+++ b/solution.py
@@ -79,7 +79,7 @@
         out_shape=jax.ShapeDtypeStruct((rows + META, width), jnp.bfloat16),
         in_specs=[vmem] * 2,
         out_specs=vmem,
-        compiler_params=pltpu.CompilerParams(vmem_limit_bytes=16 * 1024 * 1024),
+        compiler_params=pltpu.CompilerParams(vmem_limit_bytes=8 * 1024 * 1024),
     )(embeddings, numbers)
 
 
@@ -96,10 +96,15 @@
     befores = [refs.pop(0) if more else None for _, _, more in tasks]
     place = refs.pop(0) if last else None
     columns = refs.pop()
-    for name, slot in columns_of.items():
-        for index in range(sizes[name]):
+    made = set()
+
+    def column_of(name, index):
+        if (name, index) not in made:
+            made.add((name, index))
             line, _ = codes(arrays[name][index * block + rows : (index + 1) * block, :rows])
-            columns[slot + index] = jnp.broadcast_to(line, (128, rows)).T
+            columns[columns_of[name] + index] = jnp.broadcast_to(line, (128, rows)).T
+        return columns[columns_of[name] + index]
+
     done = 0
     for number, (queries, keys, _) in enumerate(tasks):
         places = [(name, index) for name in queries for index in range(sizes[name])]
@@ -116,7 +121,7 @@
                         (((1,), (1,)), ((), ())),
                         preferred_element_type=jnp.float32,
                     )
-                    column = columns[columns_of[name] + index]
+                    column = column_of(name, index)
                     column = jnp.concatenate([column] * (rows // 128), axis=1)
                     allowed = (column < code) & (column >= base)
                     scores = jnp.where(allowed, scores, -1.0).reshape(rows // 8, 8, rows)
@@ -169,16 +174,40 @@
         + [pl.BlockSpec(memory_space=pltpu.SMEM)] * last,
         out_specs=[vmem] * len(out_shape),
         scratch_shapes=[pltpu.VMEM((count, rows, 128), jnp.float32)],
-        compiler_params=pltpu.CompilerParams(vmem_limit_bytes=8 * 1024 * 1024),
+        compiler_params=pltpu.CompilerParams(vmem_limit_bytes=4 * 1024 * 1024),
         cost_estimate=pl.CostEstimate(
             flops=2 * pairs * rows * width, bytes_accessed=10000, transcendentals=0
         ),
     )(*arrays, *befores, *([place] if last else []))
 
 
+def pick_kernel(parts, block, *refs):
+    out = refs[-1]
+    for at, (name, index) in enumerate(parts):
+        out[at * block : (at + 1) * block, :] = refs[name][index * block : (index + 1) * block, :]
+
+
+def pick(parts, rows):
+    block = rows + META
+    arrays, plan = [], []
+    for value, index in parts:
+        known = [at for at, other in enumerate(arrays) if other is value]
+        if not known:
+            arrays.append(value)
+        plan.append((known[0] if known else len(arrays) - 1, index))
+    vmem = pl.BlockSpec(memory_space=pltpu.VMEM)
+    return pl.pallas_call(
+        functools.partial(pick_kernel, tuple(plan), block),
+        out_shape=jax.ShapeDtypeStruct((len(parts) * block, arrays[0].shape[1]), arrays[0].dtype),
+        in_specs=[vmem] * len(arrays),
+        out_specs=vmem,
+        compiler_params=pltpu.CompilerParams(vmem_limit_bytes=4 * 1024 * 1024),
+        cost_estimate=pl.CostEstimate(flops=0, bytes_accessed=10000, transcendentals=0),
+    )(*arrays)
+
+
 def local(embeddings, owner, cluster, order):
     rows = embeddings.shape[0]
-    block = rows + META
     index = lax.axis_index("grp")
     y, core = index // 2, index % 2
     side = 1 - 2 * core
@@ -186,27 +215,29 @@
     types = jnp.stack([core, 1 - core, core, 1 - core, 1 - core, core, core, 1 - core])
     place = (steps * 2 + types).astype(jnp.int32)
     own = prepare(embeddings, owner, cluster, order)
-    pair = jnp.concatenate([own, swap(own)], axis=0)
+    sib = swap(own)
+    sib, place = lax.optimization_barrier((sib, place))
+    pair = pick([(own, 0), (sib, 0)], rows)
     key_x = fetch(pair, 0, 1)
     key_z = fetch(pair, 2, 1)
     line_y = fetch(pair, 1, 1)
     line_2y = fetch(line_y, 1, 1)
     key_xz = fetch(key_x, 2, -1)
-    key_zx = fetch(jnp.concatenate([key_x[:block], key_z], axis=0), 0, 1)
-    key_2z = fetch(key_z[:block], 2, 1)
+    key_zx = fetch(pick([(key_x, 0), (key_z, 0), (key_z, 1)], rows), 0, 1)
     other_y = swap(line_y)
-    front, back = [pair, line_y], [other_y, line_2y]
+    front, back = [pair, line_y, other_y], [line_2y]
     near = [own, key_x, key_z]
     (best_front,) = score([(front, near, None)], rows)
+    key_2z = fetch(pick([(key_z, 0)], rows), 2, 1)
     key_xz, best_front = lax.optimization_barrier((key_xz, best_front))
     key_2x2z = jump(key_2z, 0)
     key_xzz = fetch(key_xz, 2, -1)
-    key_xxz = fetch(key_xz, 0, 1)
+    key_xxz = fetch(pick([(key_xz, 0)], rows), 0, 1)
+    far = [key_xxz, key_xzz, fetch(pick([(key_zx, 0)], rows), 2, 1), key_2x2z]
     middle = [key_xz, key_zx, key_2z]
     best_front, best_back = score(
         [(front, middle, best_front), (back, near + middle, None)], rows
     )
-    far = [key_xxz, key_xzz, key_2x2z]
     (best,) = score([(front, far, best_front), (back, far, best_back)], rows, place)
     home = lax.all_to_all(best, "grp", split_axis=0, concat_axis=0, tiled=True)
     return jnp.max(home.reshape(8, rows), axis=0)

time: 76.4 us -> 72.2 us (0.945)
  waiting for transfers between devices: 18 us -> 27.2 us
  starting transfers between devices: 21.5 us -> 17.3 us
  local copies, waits for them, and re-layouts: 4.56 us -> 1.3 us
  Pallas kernels: 18.4 us -> 15.7 us
  blocking collectives: 11 us -> 9.06 us
  other arithmetic: 2.49 us -> 1.32 us
    ppermute x12 -> x13, waiting for transfers between devices: 18 us -> 27.2 us  [permute(): return lax.ppermute(value, AXES, pairs)]
    ppermute x12 -> x13, starting transfers between devices: 21.5 us -> 17.3 us  [permute(): return lax.ppermute(value, AXES, pairs)]
    unnamed x10 -> x2, local copies, waits for them, and re-layouts: 4.33 us -> 1.13 us
    pallas_call x3, Pallas kernels: 18.2 us -> 15.3 us  [score(): pl.pallas_call(functools.partial(score_kernel, plan, sizes, columns_of, r...]
    all_to_all x1, blocking collectives: 11 us -> 9.06 us  [local(): home = lax.all_to_all(best, 'grp', split_axis=0, concat_axis=0, tiled=True)]
    concatenate x2 -> x0, other arithmetic: 1.17 us -> none  [the longest x1 1.12 us: local(): key_zx = fetch(jnp.concatenate([key_x[:block], key_z], axis=0), 0, 1)]
  transfers between devices with their start and end apart: 12 -> 13, of which waited for: 5 -> 6; matrix products, arithmetic and copies ran while one was open for 2% -> 0% of each run, Pallas kernels for 16% -> 14%
where the time goes in v3:
time: 72.2 us; the launch traced here: 72 us
  waiting for transfers between devices  27.2 us (38%)
  starting transfers between devices  17.3 us (24%)
  Pallas kernels  15.7 us (22%)
  blocking collectives  9.06 us (13%)
  other arithmetic  1.32 us (2%)
  local copies, waits for them, and re-layouts  1.3 us (2%)
    ppermute x13, waiting for transfers between devices, permute(): return lax.ppermute(value, AXES, pairs)  27.2 us
    ppermute x13, starting transfers between devices, permute(): return lax.ppermute(value, AXES, pairs)  17.3 us
    pallas_call x3, Pallas kernels, score(): pl.pallas_call(functools.partial(score_kernel, plan, sizes, columns_of, r...  15.3 us
    all_to_all x1, blocking collectives, local(): home = lax.all_to_all(best, 'grp', split_axis=0, concat_axis=0, tiled=True)  9.06 us
  transfers between devices with their start and end apart: 13, of which 6 were waited for; matrix products, arithmetic and copies ran while one was open for 0% of the time, Pallas kernels for 14%

profile of v3, /device:TPU:1, one launch (start us, length us, event | category | flops | bytes accessed | tf_op | source)
XLA Modules:
  0.0 72.0 jit_solution(17332510606358069572)
XLA Ops:
  0.0 0.7 pad_add_fusion.numbers_ref
  0.7 1.1 %copy-done = f32[256,768]{1,0:T(8,128)S(1)} copy-done((f32[256,768]{1,0:T(8,128)S(1)}, f32[256,768]{1,0:T(8,128)}, u32[]{:S(2)}) %copy-start) | copy-done | bytes 786456
  1.9 0.1 shard_map.46.refs_0_.refs_3_.refs_7_
  2.0 1.5 %collective-permute-start = (bf16[272,768]{1,0:T(8,128)(2,1)S(1)}, bf16[272,768]{1,0:T(8,128)(2,1)S(1)}, u32[]{:S(2)}, u32[]{:S(2)}) collective-permute-start(bf16[272,768]{1,0:T(8,128)(2,1)S(1)} %shard_map.46.refs_0_.refs_3_.refs_7_), channel_id=1, source_target_pairs={{0,16},{16,0},{1,17},{17,1},{2,18},{18,2},{3,19},{19,3},{32,48},{4... | collective-permute-start | bytes 1253384 | tf_op jit(solution)/shard_map/ppermute | solution.py:31
  3.5 0.1 stack.41
  3.6 0.1 stack.38
  3.7 1.2 %collective-permute-done.refs_1_ = bf16[272,768]{1,0:T(8,128)(2,1)S(1)} collective-permute-done((bf16[272,768]{1,0:T(8,128)(2,1)S(1)}, bf16[272,768]{1,0:T(8,128)(2,1)S(1)}, u32[]{:S(2)}, u32[]{:S(2)}) %collective-permute-start) | collective-permute-done | bytes 417824 | tf_op jit(solution)/shard_map/ppermute | solution.py:31
  4.9 0.1 shard_map.47.refs_0_
  4.9 1.4 %collective-permute-start.1 = (bf16[544,768]{1,0:T(8,128)(2,1)S(1)}, bf16[544,768]{1,0:T(8,128)(2,1)S(1)}, u32[]{:S(2)}, u32[]{:S(2)}) collective-permute-start(bf16[544,768]{1,0:T(8,128)(2,1)S(1)} %shard_map.47.refs_0_), channel_id=1, source_target_pairs={{0,96},{16,48},{1,97},{17,49},{2,98},{18,50},{3,99},{19,51},{32,0}... | collective-permute-start | bytes 2506760 | tf_op jit(solution)/shard_map/ppermute | solution.py:31
  6.4 1.2 %collective-permute-start.3 = (bf16[544,768]{1,0:T(8,128)(2,1)S(1)}, bf16[544,768]{1,0:T(8,128)(2,1)S(1)}, u32[]{:S(2)}, u32[]{:S(2)}) collective-permute-start(bf16[544,768]{1,0:T(8,128)(2,1)S(1)} %shard_map.47.refs_0_), channel_id=1, source_target_pairs={{0,12},{16,20},{1,13},{17,21},{2,14},{18,22},{3,15},{19,23},{32,44... | collective-permute-start | bytes 2506760 | tf_op jit(solution)/shard_map/ppermute | solution.py:31
  7.6 1.6 %collective-permute-start.5 = (bf16[544,768]{1,0:T(8,128)(2,1)S(1)}, bf16[544,768]{1,0:T(8,128)(2,1)S(1)}, u32[]{:S(2)}, u32[]{:S(2)}) collective-permute-start(bf16[544,768]{1,0:T(8,128)(2,1)S(1)} %shard_map.47.refs_0_), channel_id=1, source_target_pairs={{0,3},{16,17},{1,0},{17,18},{2,1},{18,19},{3,2},{19,16},{32,35},{4... | collective-permute-start | bytes 2506760 | tf_op jit(solution)/shard_map/ppermute | solution.py:31
  9.2 8.5 %collective-permute-done.1.refs_1_ = bf16[544,768]{1,0:T(8,128)(2,1)S(1)} collective-permute-done((bf16[544,768]{1,0:T(8,128)(2,1)S(1)}, bf16[544,768]{1,0:T(8,128)(2,1)S(1)}, u32[]{:S(2)}, u32[]{:S(2)}) %collective-permute-start.1) | collective-permute-done | bytes 835616 | tf_op jit(solution)/shard_map/ppermute | solution.py:31
  17.7 0.8 %collective-permute-start.2 = (bf16[544,768]{1,0:T(8,128)(2,1)S(1)}, bf16[544,768]{1,0:T(8,128)(2,1)S(1)}, u32[]{:S(2)}, u32[]{:S(2)}) collective-permute-start(bf16[544,768]{1,0:T(8,128)(2,1)S(1)} %collective-permute-done.1.refs_1_), channel_id=1, source_target_pairs={{0,16},{16,0},{1,17},{17,1},{2,18},{18,2},{3,19},{19,3},{32,48},{4... | collective-permute-start | bytes 2506760 | tf_op jit(solution)/shard_map/ppermute | solution.py:31
  18.5 0.5 collective-permute-done.3.refs_4_.refs_0_.refs_8_
  19.0 4.1 %collective-permute-start.4 = (bf16[544,768]{1,0:T(8,128)(2,1)S(1)}, bf16[544,768]{1,0:T(8,128)(2,1)S(1)}, u32[]{:S(2)}, u32[]{:S(2)}) collective-permute-start(bf16[544,768]{1,0:T(8,128)(2,1)S(1)} %collective-permute-done.3.refs_4_.refs_0_.refs_8_), channel_id=1, source_target_pairs={{0,1},{16,19},{1,2},{17,16},{2,3},{18,17},{3,0},{19,18},{32,33},{4... | collective-permute-start | bytes 2506760 | tf_op jit(solution)/shard_map/ppermute | solution.py:31
  23.0 0.0 collective-permute-done.5.refs_5_.refs_1_.refs_0_.refs_9_
  23.0 0.1 shard_map.50
  23.1 0.5 collective-permute-start.8
  23.7 0.9 %collective-permute-start.12 = (bf16[544,768]{1,0:T(8,128)(2,1)S(1)}, bf16[544,768]{1,0:T(8,128)(2,1)S(1)}, u32[]{:S(2)}, u32[]{:S(2)}) collective-permute-start(bf16[544,768]{1,0:T(8,128)(2,1)S(1)} %collective-permute-done.1.refs_1_), channel_id=1, source_target_pairs={{0,96},{16,48},{1,97},{17,49},{2,98},{18,50},{3,99},{19,51},{32,0}... | collective-permute-start | bytes 2506760 | tf_op jit(solution)/shard_map/ppermute | solution.py:31
  24.6 0.1 collective-permute-start.10
  24.7 3.6 %shard_map.48.refs_10_ = f32[6,8,256]{2,1,0:T(8,128)S(1)} custom-call(bf16[544,768]{1,0:T(8,128)(2,1)S(1)} %shard_map.47.refs_0_, bf16[544,768]{1,0:T(8,128)(2,1)S(1)} %collective-permute-done.1.refs_1_, bf16[544,768]{1,0:T(8,128)(2,1)S(1)} %collective-permute-done.2.refs_2_, bf16[272,768]{1,0:T(8,128)(2,1)S(1)} %shard_map.46.refs_0_.refs_3_.refs_7_, ...), custom_call_target="tpu_custom_call" | custom-call | flops 11796480 | bytes 10000 | tf_op jit(solution)/shard_map/pallas_call | solution.py:170
  28.2 7.9 %collective-permute-done.4.refs_0_.refs_3_ = bf16[544,768]{1,0:T(8,128)(2,1)S(1)} collective-permute-done((bf16[544,768]{1,0:T(8,128)(2,1)S(1)}, bf16[544,768]{1,0:T(8,128)(2,1)S(1)}, u32[]{:S(2)}, u32[]{:S(2)}) %collective-permute-start.4) | collective-permute-done | bytes 835616 | tf_op jit(solution)/shard_map/ppermute | solution.py:31
  36.2 3.4 %collective-permute-start.7 = (bf16[544,768]{1,0:T(8,128)(2,1)S(1)}, bf16[544,768]{1,0:T(8,128)(2,1)S(1)}, u32[]{:S(2)}, u32[]{:S(2)}) collective-permute-start(bf16[544,768]{1,0:T(8,128)(2,1)S(1)} %collective-permute-done.4.refs_0_.refs_3_), channel_id=1, source_target_pairs={{0,1},{16,19},{1,2},{17,16},{2,3},{18,17},{3,0},{19,18},{32,33},{4... | collective-permute-start | bytes 2506760 | tf_op jit(solution)/shard_map/ppermute | solution.py:31
  39.6 1.0 %collective-permute-start.11 = (bf16[272,768]{1,0:T(8,128)(2,1)S(1)}, bf16[272,768]{1,0:T(8,128)(2,1)S(1)}, u32[]{:S(2)}, u32[]{:S(2)}) collective-permute-start(bf16[272,768]{1,0:T(8,128)(2,1)S(1)} %collective-permute-done.10.refs_5_), channel_id=1, source_target_pairs={{0,8},{16,24},{1,9},{17,25},{2,10},{18,26},{3,11},{19,27},{32,40},... | collective-permute-start | bytes 1253384 | tf_op jit(solution)/shard_map/ppermute | solution.py:31
  40.6 0.5 collective-permute-start.6
  41.1 0.3 collective-permute-start.9
  41.4 6.6 %shard_map.53 = (f32[6,8,256]{2,1,0:T(8,128)S(1)}, f32[2,8,256]{2,1,0:T(8,128)S(1)}) custom-call(bf16[544,768]{1,0:T(8,128)(2,1)S(1)} %shard_map.47.refs_0_, bf16[544,768]{1,0:T(8,128)(2,1)S(1)} %collective-permute-done.1.refs_1_, bf16[544,768]{1,0:T(8,128)(2,1)S(1)} %collective-permute-done.2.refs_2_, ...), custom_call_target="tpu_custom_call" | custom-call | flops 22806528 | bytes 10000 | tf_op jit(solution)/shard_map/pallas_call | solution.py:170
  48.1 3.5 %collective-permute-done.11.refs_6_ = bf16[272,768]{1,0:T(8,128)(2,1)S(1)} collective-permute-done((bf16[272,768]{1,0:T(8,128)(2,1)S(1)}, bf16[272,768]{1,0:T(8,128)(2,1)S(1)}, u32[]{:S(2)}, u32[]{:S(2)}) %collective-permute-start.11) | collective-permute-done | bytes 417824 | tf_op jit(solution)/shard_map/ppermute | solution.py:31
  51.6 5.6 %collective-permute-done.6.refs_3_ = bf16[272,768]{1,0:T(8,128)(2,1)S(1)} collective-permute-done((bf16[272,768]{1,0:T(8,128)(2,1)S(1)}, bf16[272,768]{1,0:T(8,128)(2,1)S(1)}, u32[]{:S(2)}, u32[]{:S(2)}) %collective-permute-start.6) | collective-permute-done | bytes 417824 | tf_op jit(solution)/shard_map/ppermute | solution.py:31
  57.2 5.2 %shard_map.54 = f32[8,1,256]{2,1,0:T(1,128)S(1)} custom-call(bf16[544,768]{1,0:T(8,128)(2,1)S(1)} %shard_map.47.refs_0_, bf16[544,768]{1,0:T(8,128)(2,1)S(1)} %collective-permute-done.1.refs_1_, bf16[544,768]{1,0:T(8,128)(2,1)S(1)} %collective-permute-done.2.refs_2_, bf16[272,768]{1,0:T(8,128)(2,1)S(1)} %collective-permute-done.6.refs_3_, ...), custom_call_target="tpu_custom_call" | custom-call | flops 15728640 | bytes 10000 | tf_op jit(solution)/shard_map/pallas_call | solution.py:170
  62.4 9.1 %all_to_all.5 = f32[8,1,256]{2,1,0:T(1,128)S(1)} all-to-all(f32[8,1,256]{2,1,0:T(1,128)S(1)} %shard_map.54), channel_id=1, replica_groups=mesh['grp'=8,'blk'=16] {'grp'}, dimensions={0} | all-to-all | bytes 16384 | tf_op jit(solution)/shard_map/all_to_all | solution.py:242
  71.4 0.6 reduce_max.9
  (11 shorter events, 0.1 us)
Async XLA Ops:
  0.7 1.1 %copy-start = (f32[256,768]{1,0:T(8,128)S(1)}, f32[256,768]{1,0:T(8,128)}, u32[]{:S(2)}) copy-start(f32[256,768]{1,0:T(8,128)} %emb_ref.1) | copy-start | bytes 2359300
  2.0 2.9 %collective-permute-start = (bf16[272,768]{1,0:T(8,128)(2,1)S(1)}, bf16[272,768]{1,0:T(8,128)(2,1)S(1)}, u32[]{:S(2)}, u32[]{:S(2)}) collective-permute-start(bf16[272,768]{1,0:T(8,128)(2,1)S(1)} %shard_map.46.refs_0_.refs_3_.refs_7_), channel_id=1, source_target_pairs={{0,16},{16,0},{1,17},{17,1},{2,18},{18,2},{3,19},{19,3},{32,48},{4... | collective-permute-start | bytes 1253384 | tf_op jit(solution)/shard_map/ppermute | solution.py:31
  4.9 12.8 %collective-permute-start.1 = (bf16[544,768]{1,0:T(8,128)(2,1)S(1)}, bf16[544,768]{1,0:T(8,128)(2,1)S(1)}, u32[]{:S(2)}, u32[]{:S(2)}) collective-permute-start(bf16[544,768]{1,0:T(8,128)(2,1)S(1)} %shard_map.47.refs_0_), channel_id=1, source_target_pairs={{0,96},{16,48},{1,97},{17,49},{2,98},{18,50},{3,99},{19,51},{32,0}... | collective-permute-start | bytes 2506760 | tf_op jit(solution)/shard_map/ppermute | solution.py:31
  6.4 12.6 %collective-permute-start.3 = (bf16[544,768]{1,0:T(8,128)(2,1)S(1)}, bf16[544,768]{1,0:T(8,128)(2,1)S(1)}, u32[]{:S(2)}, u32[]{:S(2)}) collective-permute-start(bf16[544,768]{1,0:T(8,128)(2,1)S(1)} %shard_map.47.refs_0_), channel_id=1, source_target_pairs={{0,12},{16,20},{1,13},{17,21},{2,14},{18,22},{3,15},{19,23},{32,44... | collective-permute-start | bytes 2506760 | tf_op jit(solution)/shard_map/ppermute | solution.py:31
  7.6 15.4 %collective-permute-start.5 = (bf16[544,768]{1,0:T(8,128)(2,1)S(1)}, bf16[544,768]{1,0:T(8,128)(2,1)S(1)}, u32[]{:S(2)}, u32[]{:S(2)}) collective-permute-start(bf16[544,768]{1,0:T(8,128)(2,1)S(1)} %shard_map.47.refs_0_), channel_id=1, source_target_pairs={{0,3},{16,17},{1,0},{17,18},{2,1},{18,19},{3,2},{19,16},{32,35},{4... | collective-permute-start | bytes 2506760 | tf_op jit(solution)/shard_map/ppermute | solution.py:31
  17.7 6.9 %collective-permute-start.2 = (bf16[544,768]{1,0:T(8,128)(2,1)S(1)}, bf16[544,768]{1,0:T(8,128)(2,1)S(1)}, u32[]{:S(2)}, u32[]{:S(2)}) collective-permute-start(bf16[544,768]{1,0:T(8,128)(2,1)S(1)} %collective-permute-done.1.refs_1_), channel_id=1, source_target_pairs={{0,16},{16,0},{1,17},{17,1},{2,18},{18,2},{3,19},{19,3},{32,48},{4... | collective-permute-start | bytes 2506760 | tf_op jit(solution)/shard_map/ppermute | solution.py:31
  19.0 17.2 %collective-permute-start.4 = (bf16[544,768]{1,0:T(8,128)(2,1)S(1)}, bf16[544,768]{1,0:T(8,128)(2,1)S(1)}, u32[]{:S(2)}, u32[]{:S(2)}) collective-permute-start(bf16[544,768]{1,0:T(8,128)(2,1)S(1)} %collective-permute-done.3.refs_4_.refs_0_.refs_8_), channel_id=1, source_target_pairs={{0,1},{16,19},{1,2},{17,16},{2,3},{18,17},{3,0},{19,18},{32,33},{4... | collective-permute-start | bytes 2506760 | tf_op jit(solution)/shard_map/ppermute | solution.py:31
  23.1 18.0 %collective-permute-start.8 = (bf16[816,768]{1,0:T(8,128)(2,1)S(1)}, bf16[816,768]{1,0:T(8,128)(2,1)S(1)}, u32[]{:S(2)}, u32[]{:S(2)}) collective-permute-start(bf16[816,768]{1,0:T(8,128)(2,1)S(1)} %shard_map.50), channel_id=1, source_target_pairs={{0,12},{16,20},{1,13},{17,21},{2,14},{18,22},{3,15},{19,23},{32,44... | collective-permute-start | bytes 3760136 | tf_op jit(solution)/shard_map/ppermute | solution.py:31
  23.7 17.7 %collective-permute-start.12 = (bf16[544,768]{1,0:T(8,128)(2,1)S(1)}, bf16[544,768]{1,0:T(8,128)(2,1)S(1)}, u32[]{:S(2)}, u32[]{:S(2)}) collective-permute-start(bf16[544,768]{1,0:T(8,128)(2,1)S(1)} %collective-permute-done.1.refs_1_), channel_id=1, source_target_pairs={{0,96},{16,48},{1,97},{17,49},{2,98},{18,50},{3,99},{19,51},{32,0}... | collective-permute-start | bytes 2506760 | tf_op jit(solution)/shard_map/ppermute | solution.py:31
  24.6 15.0 %collective-permute-start.10 = (bf16[272,768]{1,0:T(8,128)(2,1)S(1)}, bf16[272,768]{1,0:T(8,128)(2,1)S(1)}, u32[]{:S(2)}, u32[]{:S(2)}) collective-permute-start(bf16[272,768]{1,0:T(8,128)(2,1)S(1)} %shard_map.52), channel_id=1, source_target_pairs={{0,3},{16,17},{1,0},{17,18},{2,1},{18,19},{3,2},{19,16},{32,35},{4... | collective-permute-start | bytes 1253384 | tf_op jit(solution)/shard_map/ppermute | solution.py:31
  36.2 21.1 %collective-permute-start.7 = (bf16[544,768]{1,0:T(8,128)(2,1)S(1)}, bf16[544,768]{1,0:T(8,128)(2,1)S(1)}, u32[]{:S(2)}, u32[]{:S(2)}) collective-permute-start(bf16[544,768]{1,0:T(8,128)(2,1)S(1)} %collective-permute-done.4.refs_0_.refs_3_), channel_id=1, source_target_pairs={{0,1},{16,19},{1,2},{17,16},{2,3},{18,17},{3,0},{19,18},{32,33},{4... | collective-permute-start | bytes 2506760 | tf_op jit(solution)/shard_map/ppermute | solution.py:31
  39.6 12.0 %collective-permute-start.11 = (bf16[272,768]{1,0:T(8,128)(2,1)S(1)}, bf16[272,768]{1,0:T(8,128)(2,1)S(1)}, u32[]{:S(2)}, u32[]{:S(2)}) collective-permute-start(bf16[272,768]{1,0:T(8,128)(2,1)S(1)} %collective-permute-done.10.refs_5_), channel_id=1, source_target_pairs={{0,8},{16,24},{1,9},{17,25},{2,10},{18,26},{3,11},{19,27},{32,40},... | collective-permute-start | bytes 1253384 | tf_op jit(solution)/shard_map/ppermute | solution.py:31
  40.6 16.6 %collective-permute-start.6 = (bf16[272,768]{1,0:T(8,128)(2,1)S(1)}, bf16[272,768]{1,0:T(8,128)(2,1)S(1)}, u32[]{:S(2)}, u32[]{:S(2)}) collective-permute-start(bf16[272,768]{1,0:T(8,128)(2,1)S(1)} %shard_map.49), channel_id=1, source_target_pairs={{0,12},{16,20},{1,13},{17,21},{2,14},{18,22},{3,15},{19,23},{32,44... | collective-permute-start | bytes 1253384 | tf_op jit(solution)/shard_map/ppermute | solution.py:31
  41.1 16.1 %collective-permute-start.9 = (bf16[272,768]{1,0:T(8,128)(2,1)S(1)}, bf16[272,768]{1,0:T(8,128)(2,1)S(1)}, u32[]{:S(2)}, u32[]{:S(2)}) collective-permute-start(bf16[272,768]{1,0:T(8,128)(2,1)S(1)} %shard_map.51), channel_id=1, source_target_pairs={{0,3},{16,17},{1,0},{17,18},{2,1},{18,19},{3,2},{19,16},{32,35},{4... | collective-permute-start | bytes 1253384 | tf_op jit(solution)/shard_map/ppermute | solution.py:31

commit v4 on v3

--- a/solution.py
+++ b/solution.py
@@ -53,7 +53,7 @@
     return permute(value, lambda core: (0, 0, 0, 1))
 
 
-def prepare_kernel(emb_ref, numbers_ref, out_ref):
+def write_block(emb_ref, numbers_ref, out_ref, start):
     rows, width = emb_ref.shape
     owner, cluster, order = numbers_ref[0:1, :], numbers_ref[1:2, :], numbers_ref[2:3, :]
     high = jnp.right_shift(order, 8)
@@ -61,11 +61,22 @@
     ident = owner * 2 + cluster
     line = lax.broadcasted_iota(jnp.int32, (META, rows), 0)
     meta = jnp.where(line == 0, high, jnp.where(line == 1, low, jnp.where(line == 2, ident, 0)))
-    out_ref[rows:, :] = jnp.zeros((META, width), jnp.bfloat16)
-    out_ref[rows:, :rows] = meta.astype(jnp.float32).astype(jnp.bfloat16)
+    end = start + rows
+    out_ref[end : end + META, :] = jnp.zeros((META, width), jnp.bfloat16)
+    out_ref[end : end + META, :rows] = meta.astype(jnp.float32).astype(jnp.bfloat16)
     values = emb_ref[...]
     scale = lax.rsqrt(jnp.sum(values * values, axis=1, keepdims=True) + 1e-06)
-    out_ref[:rows, :] = (values * scale).astype(jnp.bfloat16)
+    out_ref[start:end, :] = (values * scale).astype(jnp.bfloat16)
+
+
+def own_kernel(emb_ref, numbers_ref, out_ref):
+    write_block(emb_ref, numbers_ref, out_ref, 0)
+
+
+def pair_kernel(own_ref, emb_ref, numbers_ref, out_ref):
+    block = own_ref.shape[0]
+    out_ref[:block, :] = own_ref[...]
+    write_block(emb_ref, numbers_ref, out_ref, block)
 
 
 def prepare(embeddings, owner, cluster, order):
@@ -74,13 +85,25 @@
     numbers = jnp.concatenate(
         [owner.reshape(1, rows), cluster.reshape(1, rows), order.reshape(1, rows)], axis=0
     )
-    return pl.pallas_call(
-        prepare_kernel,
+    other, other_numbers = swap(embeddings), swap(numbers)
+    params = pltpu.CompilerParams(vmem_limit_bytes=8 * 1024 * 1024)
+    own = pl.pallas_call(
+        own_kernel,
         out_shape=jax.ShapeDtypeStruct((rows + META, width), jnp.bfloat16),
         in_specs=[vmem] * 2,
         out_specs=vmem,
-        compiler_params=pltpu.CompilerParams(vmem_limit_bytes=8 * 1024 * 1024),
+        compiler_params=params,
+        cost_estimate=pl.CostEstimate(flops=0, bytes_accessed=10000, transcendentals=0),
     )(embeddings, numbers)
+    pair = pl.pallas_call(
+        pair_kernel,
+        out_shape=jax.ShapeDtypeStruct((2 * (rows + META), width), jnp.bfloat16),
+        in_specs=[vmem] * 3,
+        out_specs=vmem,
+        compiler_params=params,
+        cost_estimate=pl.CostEstimate(flops=0, bytes_accessed=10000, transcendentals=0),
+    )(own, other, other_numbers)
+    return own, pair
 
 
 def codes(meta):
@@ -214,10 +237,8 @@
     steps = jnp.stack([y, y, y + side, y + side, y - side, y - side, y + 2, y + 2]) % GRID
     types = jnp.stack([core, 1 - core, core, 1 - core, 1 - core, core, core, 1 - core])
     place = (steps * 2 + types).astype(jnp.int32)
-    own = prepare(embeddings, owner, cluster, order)
-    sib = swap(own)
-    sib, place = lax.optimization_barrier((sib, place))
-    pair = pick([(own, 0), (sib, 0)], rows)
+    own, pair = prepare(embeddings, owner, cluster, order)
+    pair, place = lax.optimization_barrier((pair, place))
     key_x = fetch(pair, 0, 1)
     key_z = fetch(pair, 2, 1)
     line_y = fetch(pair, 1, 1)

time: 72.2 us -> 71.2 us (0.986)
  waiting for transfers between devices: 27.2 us -> 26 us
    ppermute x13 -> x14, waiting for transfers between devices: 27.2 us -> 26 us  [permute(): return lax.ppermute(value, AXES, pairs)]
    ppermute x13 -> x14, starting transfers between devices: 17.3 us -> 17.3 us  [permute(): return lax.ppermute(value, AXES, pairs)]
  transfers between devices with their start and end apart: 13 -> 14, of which waited for: 6 -> 5; matrix products, arithmetic and copies ran while one was open for 0% -> 1% of each run, Pallas kernels for 14% -> 15%
where the time goes in v4:
time: 71.2 us; the launch traced here: 71 us
  waiting for transfers between devices  26 us (37%)
  starting transfers between devices  17.3 us (24%)
  Pallas kernels  15.8 us (22%)
  blocking collectives  9.08 us (13%)
  other arithmetic  1.32 us (2%)
  local copies, waits for them, and re-layouts  1.3 us (2%)
    ppermute x14, waiting for transfers between devices, permute(): return lax.ppermute(value, AXES, pairs)  26 us
    ppermute x14, starting transfers between devices, permute(): return lax.ppermute(value, AXES, pairs)  17.3 us
    pallas_call x3, Pallas kernels, score(): pl.pallas_call(functools.partial(score_kernel, plan, sizes, columns_of, r...  15.4 us
    all_to_all x1, blocking collectives, local(): home = lax.all_to_all(best, 'grp', split_axis=0, concat_axis=0, tiled=True)  9.08 us
  transfers between devices with their start and end apart: 14, of which 5 were waited for; matrix products, arithmetic and copies ran while one was open for 1% of the time, Pallas kernels for 15%

profile of v4, /device:TPU:1, one launch (start us, length us, event | category | flops | bytes accessed | tf_op | source)
XLA Modules:
  0.0 71.0 jit_solution(18216738714808857253)
XLA Ops:
  0.0 1.4 %collective-permute-start = (f32[256,768]{1,0:T(8,128)}, f32[256,768]{1,0:T(8,128)S(1)}, u32[]{:S(2)}, u32[]{:S(2)}) collective-permute-start(f32[256,768]{1,0:T(8,128)} %emb_ref.1), channel_id=1, source_target_pairs={{0,16},{16,0},{1,17},{17,1},{2,18},{18,2},{3,19},{19,3},{32,48},{4... | collective-permute-start | bytes 2359304 | tf_op jit(solution)/shard_map/ppermute | solution.py:31
  1.4 0.7 %pad_add_fusion.numbers_ref = s32[3,256]{1,0:T(4,128)S(1)} fusion(s32[1,256]{1,0:T(1,128)} %bitcast.9, s32[1,256]{1,0:T(1,128)} %bitcast.10, s32[1,256]{1,0:T(1,128)} %bitcast.11), kind=kLoop, calls=%fused_computation | loop fusion | flops 1536 | bytes 6144 | tf_op jit(solution)/shard_map/concatenate | solution.py:85
  2.1 0.0 collective-permute-start.1
  2.2 0.1 stack.41
  2.3 0.1 stack.38
  2.4 1.1 %copy-done = f32[256,768]{1,0:T(8,128)S(1)} copy-done((f32[256,768]{1,0:T(8,128)S(1)}, f32[256,768]{1,0:T(8,128)}, u32[]{:S(2)}) %copy-start) | copy-done | bytes 786456
  3.5 0.1 shard_map.46.own_ref.refs_3_.refs_7_
  3.7 0.0 collective-permute-done.emb_ref
  3.7 0.1 shard_map.47.refs_0_
  3.8 1.4 %collective-permute-start.2 = (bf16[544,768]{1,0:T(8,128)(2,1)S(1)}, bf16[544,768]{1,0:T(8,128)(2,1)S(1)}, u32[]{:S(2)}, u32[]{:S(2)}) collective-permute-start(bf16[544,768]{1,0:T(8,128)(2,1)S(1)} %shard_map.47.refs_0_), channel_id=1, source_target_pairs={{0,96},{16,48},{1,97},{17,49},{2,98},{18,50},{3,99},{19,51},{32,0}... | collective-permute-start | bytes 2506760 | tf_op jit(solution)/shard_map/ppermute | solution.py:31
  5.3 1.2 %collective-permute-start.4 = (bf16[544,768]{1,0:T(8,128)(2,1)S(1)}, bf16[544,768]{1,0:T(8,128)(2,1)S(1)}, u32[]{:S(2)}, u32[]{:S(2)}) collective-permute-start(bf16[544,768]{1,0:T(8,128)(2,1)S(1)} %shard_map.47.refs_0_), channel_id=1, source_target_pairs={{0,12},{16,20},{1,13},{17,21},{2,14},{18,22},{3,15},{19,23},{32,44... | collective-permute-start | bytes 2506760 | tf_op jit(solution)/shard_map/ppermute | solution.py:31
  6.5 1.6 %collective-permute-start.6 = (bf16[544,768]{1,0:T(8,128)(2,1)S(1)}, bf16[544,768]{1,0:T(8,128)(2,1)S(1)}, u32[]{:S(2)}, u32[]{:S(2)}) collective-permute-start(bf16[544,768]{1,0:T(8,128)(2,1)S(1)} %shard_map.47.refs_0_), channel_id=1, source_target_pairs={{0,3},{16,17},{1,0},{17,18},{2,1},{18,19},{3,2},{19,16},{32,35},{4... | collective-permute-start | bytes 2506760 | tf_op jit(solution)/shard_map/ppermute | solution.py:31
  8.1 8.5 %collective-permute-done.2.refs_1_ = bf16[544,768]{1,0:T(8,128)(2,1)S(1)} collective-permute-done((bf16[544,768]{1,0:T(8,128)(2,1)S(1)}, bf16[544,768]{1,0:T(8,128)(2,1)S(1)}, u32[]{:S(2)}, u32[]{:S(2)}) %collective-permute-start.2) | collective-permute-done | bytes 835616 | tf_op jit(solution)/shard_map/ppermute | solution.py:31
  16.6 0.9 %collective-permute-start.3 = (bf16[544,768]{1,0:T(8,128)(2,1)S(1)}, bf16[544,768]{1,0:T(8,128)(2,1)S(1)}, u32[]{:S(2)}, u32[]{:S(2)}) collective-permute-start(bf16[544,768]{1,0:T(8,128)(2,1)S(1)} %collective-permute-done.2.refs_1_), channel_id=1, source_target_pairs={{0,16},{16,0},{1,17},{17,1},{2,18},{18,2},{3,19},{19,3},{32,48},{4... | collective-permute-start | bytes 2506760 | tf_op jit(solution)/shard_map/ppermute | solution.py:31
  17.5 0.3 collective-permute-done.4.refs_4_.refs_0_.refs_8_
  17.8 4.1 %collective-permute-start.5 = (bf16[544,768]{1,0:T(8,128)(2,1)S(1)}, bf16[544,768]{1,0:T(8,128)(2,1)S(1)}, u32[]{:S(2)}, u32[]{:S(2)}) collective-permute-start(bf16[544,768]{1,0:T(8,128)(2,1)S(1)} %collective-permute-done.4.refs_4_.refs_0_.refs_8_), channel_id=1, source_target_pairs={{0,1},{16,19},{1,2},{17,16},{2,3},{18,17},{3,0},{19,18},{32,33},{4... | collective-permute-start | bytes 2506760 | tf_op jit(solution)/shard_map/ppermute | solution.py:31
  21.9 0.1 shard_map.50
  22.0 0.6 collective-permute-start.9
  22.6 0.8 %collective-permute-start.13 = (bf16[544,768]{1,0:T(8,128)(2,1)S(1)}, bf16[544,768]{1,0:T(8,128)(2,1)S(1)}, u32[]{:S(2)}, u32[]{:S(2)}) collective-permute-start(bf16[544,768]{1,0:T(8,128)(2,1)S(1)} %collective-permute-done.2.refs_1_), channel_id=1, source_target_pairs={{0,96},{16,48},{1,97},{17,49},{2,98},{18,50},{3,99},{19,51},{32,0}... | collective-permute-start | bytes 2506760 | tf_op jit(solution)/shard_map/ppermute | solution.py:31
  23.5 0.1 collective-permute-start.11
  23.6 3.6 %shard_map.48.refs_10_ = f32[6,8,256]{2,1,0:T(8,128)S(1)} custom-call(bf16[544,768]{1,0:T(8,128)(2,1)S(1)} %shard_map.47.refs_0_, bf16[544,768]{1,0:T(8,128)(2,1)S(1)} %collective-permute-done.2.refs_1_, bf16[544,768]{1,0:T(8,128)(2,1)S(1)} %collective-permute-done.3.refs_2_, bf16[272,768]{1,0:T(8,128)(2,1)S(1)} %shard_map.46.own_ref.refs_3_.refs_7_, ...), custom_call_target="tpu_custom_call" | custom-call | flops 11796480 | bytes 10000 | tf_op jit(solution)/shard_map/pallas_call | solution.py:193
  27.1 8.0 %collective-permute-done.5.refs_0_.refs_3_ = bf16[544,768]{1,0:T(8,128)(2,1)S(1)} collective-permute-done((bf16[544,768]{1,0:T(8,128)(2,1)S(1)}, bf16[544,768]{1,0:T(8,128)(2,1)S(1)}, u32[]{:S(2)}, u32[]{:S(2)}) %collective-permute-start.5) | collective-permute-done | bytes 835616 | tf_op jit(solution)/shard_map/ppermute | solution.py:31
  35.1 3.4 %collective-permute-start.8 = (bf16[544,768]{1,0:T(8,128)(2,1)S(1)}, bf16[544,768]{1,0:T(8,128)(2,1)S(1)}, u32[]{:S(2)}, u32[]{:S(2)}) collective-permute-start(bf16[544,768]{1,0:T(8,128)(2,1)S(1)} %collective-permute-done.5.refs_0_.refs_3_), channel_id=1, source_target_pairs={{0,1},{16,19},{1,2},{17,16},{2,3},{18,17},{3,0},{19,18},{32,33},{4... | collective-permute-start | bytes 2506760 | tf_op jit(solution)/shard_map/ppermute | solution.py:31
  38.6 1.0 %collective-permute-start.12 = (bf16[272,768]{1,0:T(8,128)(2,1)S(1)}, bf16[272,768]{1,0:T(8,128)(2,1)S(1)}, u32[]{:S(2)}, u32[]{:S(2)}) collective-permute-start(bf16[272,768]{1,0:T(8,128)(2,1)S(1)} %collective-permute-done.11.refs_5_), channel_id=1, source_target_pairs={{0,8},{16,24},{1,9},{17,25},{2,10},{18,26},{3,11},{19,27},{32,40},... | collective-permute-start | bytes 1253384 | tf_op jit(solution)/shard_map/ppermute | solution.py:31
  39.6 0.5 collective-permute-start.7
  40.1 0.3 collective-permute-start.10
  40.4 6.7 %shard_map.53 = (f32[6,8,256]{2,1,0:T(8,128)S(1)}, f32[2,8,256]{2,1,0:T(8,128)S(1)}) custom-call(bf16[544,768]{1,0:T(8,128)(2,1)S(1)} %shard_map.47.refs_0_, bf16[544,768]{1,0:T(8,128)(2,1)S(1)} %collective-permute-done.2.refs_1_, bf16[544,768]{1,0:T(8,128)(2,1)S(1)} %collective-permute-done.3.refs_2_, ...), custom_call_target="tpu_custom_call" | custom-call | flops 22806528 | bytes 10000 | tf_op jit(solution)/shard_map/pallas_call | solution.py:193
  47.0 3.5 %collective-permute-done.12.refs_6_ = bf16[272,768]{1,0:T(8,128)(2,1)S(1)} collective-permute-done((bf16[272,768]{1,0:T(8,128)(2,1)S(1)}, bf16[272,768]{1,0:T(8,128)(2,1)S(1)}, u32[]{:S(2)}, u32[]{:S(2)}) %collective-permute-start.12) | collective-permute-done | bytes 417824 | tf_op jit(solution)/shard_map/ppermute | solution.py:31
  50.6 5.6 %collective-permute-done.7.refs_3_ = bf16[272,768]{1,0:T(8,128)(2,1)S(1)} collective-permute-done((bf16[272,768]{1,0:T(8,128)(2,1)S(1)}, bf16[272,768]{1,0:T(8,128)(2,1)S(1)}, u32[]{:S(2)}, u32[]{:S(2)}) %collective-permute-start.7) | collective-permute-done | bytes 417824 | tf_op jit(solution)/shard_map/ppermute | solution.py:31
  56.2 5.1 %shard_map.54 = f32[8,1,256]{2,1,0:T(1,128)S(1)} custom-call(bf16[544,768]{1,0:T(8,128)(2,1)S(1)} %shard_map.47.refs_0_, bf16[544,768]{1,0:T(8,128)(2,1)S(1)} %collective-permute-done.2.refs_1_, bf16[544,768]{1,0:T(8,128)(2,1)S(1)} %collective-permute-done.3.refs_2_, bf16[272,768]{1,0:T(8,128)(2,1)S(1)} %collective-permute-done.7.refs_3_, ...), custom_call_target="tpu_custom_call" | custom-call | flops 15728640 | bytes 10000 | tf_op jit(solution)/shard_map/pallas_call | solution.py:193
  61.4 9.1 %all_to_all.5 = f32[8,1,256]{2,1,0:T(1,128)S(1)} all-to-all(f32[8,1,256]{2,1,0:T(1,128)S(1)} %shard_map.54), channel_id=1, replica_groups=mesh['grp'=8,'blk'=16] {'grp'}, dimensions={0} | all-to-all | bytes 16384 | tf_op jit(solution)/shard_map/all_to_all | solution.py:263
  70.4 0.6 reduce_max.9
  (13 shorter events, 0.1 us)
Async XLA Ops:
  0.0 3.7 %collective-permute-start = (f32[256,768]{1,0:T(8,128)}, f32[256,768]{1,0:T(8,128)S(1)}, u32[]{:S(2)}, u32[]{:S(2)}) collective-permute-start(f32[256,768]{1,0:T(8,128)} %emb_ref.1), channel_id=1, source_target_pairs={{0,16},{16,0},{1,17},{17,1},{2,18},{18,2},{3,19},{19,3},{32,48},{4... | collective-permute-start | bytes 2359304 | tf_op jit(solution)/shard_map/ppermute | solution.py:31
  2.1 1.5 %collective-permute-start.1 = (s32[3,256]{1,0:T(4,128)S(1)}, s32[3,256]{1,0:T(4,128)S(1)}, u32[]{:S(2)}, u32[]{:S(2)}) collective-permute-start(s32[3,256]{1,0:T(4,128)S(1)} %pad_add_fusion.numbers_ref), channel_id=1, source_target_pairs={{0,16},{16,0},{1,17},{17,1},{2,18},{18,2},{3,19},{19,3},{32,48},{4... | collective-permute-start | bytes 9224 | tf_op jit(solution)/shard_map/ppermute | solution.py:31
  2.4 1.1 %copy-start = (f32[256,768]{1,0:T(8,128)S(1)}, f32[256,768]{1,0:T(8,128)}, u32[]{:S(2)}) copy-start(f32[256,768]{1,0:T(8,128)} %emb_ref.1) | copy-start | bytes 2359300
  3.8 12.8 %collective-permute-start.2 = (bf16[544,768]{1,0:T(8,128)(2,1)S(1)}, bf16[544,768]{1,0:T(8,128)(2,1)S(1)}, u32[]{:S(2)}, u32[]{:S(2)}) collective-permute-start(bf16[544,768]{1,0:T(8,128)(2,1)S(1)} %shard_map.47.refs_0_), channel_id=1, source_target_pairs={{0,96},{16,48},{1,97},{17,49},{2,98},{18,50},{3,99},{19,51},{32,0}... | collective-permute-start | bytes 2506760 | tf_op jit(solution)/shard_map/ppermute | solution.py:31
  5.3 12.6 %collective-permute-start.4 = (bf16[544,768]{1,0:T(8,128)(2,1)S(1)}, bf16[544,768]{1,0:T(8,128)(2,1)S(1)}, u32[]{:S(2)}, u32[]{:S(2)}) collective-permute-start(bf16[544,768]{1,0:T(8,128)(2,1)S(1)} %shard_map.47.refs_0_), channel_id=1, source_target_pairs={{0,12},{16,20},{1,13},{17,21},{2,14},{18,22},{3,15},{19,23},{32,44... | collective-permute-start | bytes 2506760 | tf_op jit(solution)/shard_map/ppermute | solution.py:31
  6.5 15.4 %collective-permute-start.6 = (bf16[544,768]{1,0:T(8,128)(2,1)S(1)}, bf16[544,768]{1,0:T(8,128)(2,1)S(1)}, u32[]{:S(2)}, u32[]{:S(2)}) collective-permute-start(bf16[544,768]{1,0:T(8,128)(2,1)S(1)} %shard_map.47.refs_0_), channel_id=1, source_target_pairs={{0,3},{16,17},{1,0},{17,18},{2,1},{18,19},{3,2},{19,16},{32,35},{4... | collective-permute-start | bytes 2506760 | tf_op jit(solution)/shard_map/ppermute | solution.py:31
  16.6 6.9 %collective-permute-start.3 = (bf16[544,768]{1,0:T(8,128)(2,1)S(1)}, bf16[544,768]{1,0:T(8,128)(2,1)S(1)}, u32[]{:S(2)}, u32[]{:S(2)}) collective-permute-start(bf16[544,768]{1,0:T(8,128)(2,1)S(1)} %collective-permute-done.2.refs_1_), channel_id=1, source_target_pairs={{0,16},{16,0},{1,17},{17,1},{2,18},{18,2},{3,19},{19,3},{32,48},{4... | collective-permute-start | bytes 2506760 | tf_op jit(solution)/shard_map/ppermute | solution.py:31
  17.8 17.3 %collective-permute-start.5 = (bf16[544,768]{1,0:T(8,128)(2,1)S(1)}, bf16[544,768]{1,0:T(8,128)(2,1)S(1)}, u32[]{:S(2)}, u32[]{:S(2)}) collective-permute-start(bf16[544,768]{1,0:T(8,128)(2,1)S(1)} %collective-permute-done.4.refs_4_.refs_0_.refs_8_), channel_id=1, source_target_pairs={{0,1},{16,19},{1,2},{17,16},{2,3},{18,17},{3,0},{19,18},{32,33},{4... | collective-permute-start | bytes 2506760 | tf_op jit(solution)/shard_map/ppermute | solution.py:31
  22.0 18.1 %collective-permute-start.9 = (bf16[816,768]{1,0:T(8,128)(2,1)S(1)}, bf16[816,768]{1,0:T(8,128)(2,1)S(1)}, u32[]{:S(2)}, u32[]{:S(2)}) collective-permute-start(bf16[816,768]{1,0:T(8,128)(2,1)S(1)} %shard_map.50), channel_id=1, source_target_pairs={{0,12},{16,20},{1,13},{17,21},{2,14},{18,22},{3,15},{19,23},{32,44... | collective-permute-start | bytes 3760136 | tf_op jit(solution)/shard_map/ppermute | solution.py:31
  22.6 17.7 %collective-permute-start.13 = (bf16[544,768]{1,0:T(8,128)(2,1)S(1)}, bf16[544,768]{1,0:T(8,128)(2,1)S(1)}, u32[]{:S(2)}, u32[]{:S(2)}) collective-permute-start(bf16[544,768]{1,0:T(8,128)(2,1)S(1)} %collective-permute-done.2.refs_1_), channel_id=1, source_target_pairs={{0,96},{16,48},{1,97},{17,49},{2,98},{18,50},{3,99},{19,51},{32,0}... | collective-permute-start | bytes 2506760 | tf_op jit(solution)/shard_map/ppermute | solution.py:31
  23.5 15.1 %collective-permute-start.11 = (bf16[272,768]{1,0:T(8,128)(2,1)S(1)}, bf16[272,768]{1,0:T(8,128)(2,1)S(1)}, u32[]{:S(2)}, u32[]{:S(2)}) collective-permute-start(bf16[272,768]{1,0:T(8,128)(2,1)S(1)} %shard_map.52), channel_id=1, source_target_pairs={{0,3},{16,17},{1,0},{17,18},{2,1},{18,19},{3,2},{19,16},{32,35},{4... | collective-permute-start | bytes 1253384 | tf_op jit(solution)/shard_map/ppermute | solution.py:31
  35.1 21.1 %collective-permute-start.8 = (bf16[544,768]{1,0:T(8,128)(2,1)S(1)}, bf16[544,768]{1,0:T(8,128)(2,1)S(1)}, u32[]{:S(2)}, u32[]{:S(2)}) collective-permute-start(bf16[544,768]{1,0:T(8,128)(2,1)S(1)} %collective-permute-done.5.refs_0_.refs_3_), channel_id=1, source_target_pairs={{0,1},{16,19},{1,2},{17,16},{2,3},{18,17},{3,0},{19,18},{32,33},{4... | collective-permute-start | bytes 2506760 | tf_op jit(solution)/shard_map/ppermute | solution.py:31
  38.6 12.0 %collective-permute-start.12 = (bf16[272,768]{1,0:T(8,128)(2,1)S(1)}, bf16[272,768]{1,0:T(8,128)(2,1)S(1)}, u32[]{:S(2)}, u32[]{:S(2)}) collective-permute-start(bf16[272,768]{1,0:T(8,128)(2,1)S(1)} %collective-permute-done.11.refs_5_), channel_id=1, source_target_pairs={{0,8},{16,24},{1,9},{17,25},{2,10},{18,26},{3,11},{19,27},{32,40},... | collective-permute-start | bytes 1253384 | tf_op jit(solution)/shard_map/ppermute | solution.py:31
  39.6 16.6 %collective-permute-start.7 = (bf16[272,768]{1,0:T(8,128)(2,1)S(1)}, bf16[272,768]{1,0:T(8,128)(2,1)S(1)}, u32[]{:S(2)}, u32[]{:S(2)}) collective-permute-start(bf16[272,768]{1,0:T(8,128)(2,1)S(1)} %shard_map.49), channel_id=1, source_target_pairs={{0,12},{16,20},{1,13},{17,21},{2,14},{18,22},{3,15},{19,23},{32,44... | collective-permute-start | bytes 1253384 | tf_op jit(solution)/shard_map/ppermute | solution.py:31
  40.1 16.1 %collective-permute-start.10 = (bf16[272,768]{1,0:T(8,128)(2,1)S(1)}, bf16[272,768]{1,0:T(8,128)(2,1)S(1)}, u32[]{:S(2)}, u32[]{:S(2)}) collective-permute-start(bf16[272,768]{1,0:T(8,128)(2,1)S(1)} %shard_map.51), channel_id=1, source_target_pairs={{0,3},{16,17},{1,0},{17,18},{2,1},{18,19},{3,2},{19,16},{32,35},{4... | collective-permute-start | bytes 1253384 | tf_op jit(solution)/shard_map/ppermute | solution.py:31

commit v5 on v4

--- a/solution.py
+++ b/solution.py
@@ -242,10 +242,11 @@
     key_x = fetch(pair, 0, 1)
     key_z = fetch(pair, 2, 1)
     line_y = fetch(pair, 1, 1)
-    line_2y = fetch(line_y, 1, 1)
     key_xz = fetch(key_x, 2, -1)
     key_zx = fetch(pick([(key_x, 0), (key_z, 0), (key_z, 1)], rows), 0, 1)
     other_y = swap(line_y)
+    line_y_later, other_y = lax.optimization_barrier((line_y, other_y))
+    line_2y = fetch(line_y_later, 1, 1)
     front, back = [pair, line_y, other_y], [line_2y]
     near = [own, key_x, key_z]
     (best_front,) = score([(front, near, None)], rows)

time: 71.2 us -> 71.2 us (level)
  no operation moved by 1% of the time
where the time goes in v5:
time: 71.2 us; the launch traced here: 71 us
  waiting for transfers between devices  26.1 us (37%)
  starting transfers between devices  17.3 us (24%)
  Pallas kernels  15.8 us (22%)
  blocking collectives  9.08 us (13%)
  other arithmetic  1.32 us (2%)
  local copies, waits for them, and re-layouts  1.3 us (2%)
    ppermute x14, waiting for transfers between devices, permute(): return lax.ppermute(value, AXES, pairs)  26.1 us
    ppermute x14, starting transfers between devices, permute(): return lax.ppermute(value, AXES, pairs)  17.3 us
    pallas_call x3, Pallas kernels, score(): pl.pallas_call(functools.partial(score_kernel, plan, sizes, columns_of, r...  15.4 us
    all_to_all x1, blocking collectives, local(): home = lax.all_to_all(best, 'grp', split_axis=0, concat_axis=0, tiled=True)  9.08 us
  transfers between devices with their start and end apart: 14, of which 5 were waited for; matrix products, arithmetic and copies ran while one was open for 1% of the time, Pallas kernels for 15%

profile of v5, /device:TPU:1, one launch (start us, length us, event | category | flops | bytes accessed | tf_op | source)
XLA Modules:
  0.0 71.0 jit_solution(582450697273458241)
XLA Ops:
  0.0 1.4 %collective-permute-start = (f32[256,768]{1,0:T(8,128)}, f32[256,768]{1,0:T(8,128)S(1)}, u32[]{:S(2)}, u32[]{:S(2)}) collective-permute-start(f32[256,768]{1,0:T(8,128)} %emb_ref.1), channel_id=1, source_target_pairs={{0,16},{16,0},{1,17},{17,1},{2,18},{18,2},{3,19},{19,3},{32,48},{4... | collective-permute-start | bytes 2359304 | tf_op jit(solution)/shard_map/ppermute | solution.py:31
  1.4 0.7 %pad_add_fusion.numbers_ref = s32[3,256]{1,0:T(4,128)S(1)} fusion(s32[1,256]{1,0:T(1,128)} %bitcast.9, s32[1,256]{1,0:T(1,128)} %bitcast.10, s32[1,256]{1,0:T(1,128)} %bitcast.11), kind=kLoop, calls=%fused_computation | loop fusion | flops 1536 | bytes 6144 | tf_op jit(solution)/shard_map/concatenate | solution.py:85
  2.1 0.0 collective-permute-start.1
  2.2 0.1 stack.41
  2.3 0.1 stack.38
  2.4 1.1 %copy-done = f32[256,768]{1,0:T(8,128)S(1)} copy-done((f32[256,768]{1,0:T(8,128)S(1)}, f32[256,768]{1,0:T(8,128)}, u32[]{:S(2)}) %copy-start) | copy-done | bytes 786456
  3.5 0.1 shard_map.46.own_ref.refs_3_.refs_7_
  3.7 0.0 collective-permute-done.emb_ref
  3.7 0.1 shard_map.47.refs_0_
  3.8 1.4 %collective-permute-start.2 = (bf16[544,768]{1,0:T(8,128)(2,1)S(1)}, bf16[544,768]{1,0:T(8,128)(2,1)S(1)}, u32[]{:S(2)}, u32[]{:S(2)}) collective-permute-start(bf16[544,768]{1,0:T(8,128)(2,1)S(1)} %shard_map.47.refs_0_), channel_id=1, source_target_pairs={{0,96},{16,48},{1,97},{17,49},{2,98},{18,50},{3,99},{19,51},{32,0}... | collective-permute-start | bytes 2506760 | tf_op jit(solution)/shard_map/ppermute | solution.py:31
  5.3 1.2 %collective-permute-start.4 = (bf16[544,768]{1,0:T(8,128)(2,1)S(1)}, bf16[544,768]{1,0:T(8,128)(2,1)S(1)}, u32[]{:S(2)}, u32[]{:S(2)}) collective-permute-start(bf16[544,768]{1,0:T(8,128)(2,1)S(1)} %shard_map.47.refs_0_), channel_id=1, source_target_pairs={{0,12},{16,20},{1,13},{17,21},{2,14},{18,22},{3,15},{19,23},{32,44... | collective-permute-start | bytes 2506760 | tf_op jit(solution)/shard_map/ppermute | solution.py:31
  6.5 1.6 %collective-permute-start.6 = (bf16[544,768]{1,0:T(8,128)(2,1)S(1)}, bf16[544,768]{1,0:T(8,128)(2,1)S(1)}, u32[]{:S(2)}, u32[]{:S(2)}) collective-permute-start(bf16[544,768]{1,0:T(8,128)(2,1)S(1)} %shard_map.47.refs_0_), channel_id=1, source_target_pairs={{0,3},{16,17},{1,0},{17,18},{2,1},{18,19},{3,2},{19,16},{32,35},{4... | collective-permute-start | bytes 2506760 | tf_op jit(solution)/shard_map/ppermute | solution.py:31
  8.1 8.5 %collective-permute-done.2.refs_1_ = bf16[544,768]{1,0:T(8,128)(2,1)S(1)} collective-permute-done((bf16[544,768]{1,0:T(8,128)(2,1)S(1)}, bf16[544,768]{1,0:T(8,128)(2,1)S(1)}, u32[]{:S(2)}, u32[]{:S(2)}) %collective-permute-start.2) | collective-permute-done | bytes 835616 | tf_op jit(solution)/shard_map/ppermute | solution.py:31
  16.6 0.9 %collective-permute-start.3 = (bf16[544,768]{1,0:T(8,128)(2,1)S(1)}, bf16[544,768]{1,0:T(8,128)(2,1)S(1)}, u32[]{:S(2)}, u32[]{:S(2)}) collective-permute-start(bf16[544,768]{1,0:T(8,128)(2,1)S(1)} %collective-permute-done.2.refs_1_), channel_id=1, source_target_pairs={{0,16},{16,0},{1,17},{17,1},{2,18},{18,2},{3,19},{19,3},{32,48},{4... | collective-permute-start | bytes 2506760 | tf_op jit(solution)/shard_map/ppermute | solution.py:31
  17.5 0.3 collective-permute-done.4.refs_4_.refs_0_.refs_8_
  17.8 4.1 %collective-permute-start.5 = (bf16[544,768]{1,0:T(8,128)(2,1)S(1)}, bf16[544,768]{1,0:T(8,128)(2,1)S(1)}, u32[]{:S(2)}, u32[]{:S(2)}) collective-permute-start(bf16[544,768]{1,0:T(8,128)(2,1)S(1)} %collective-permute-done.4.refs_4_.refs_0_.refs_8_), channel_id=1, source_target_pairs={{0,1},{16,19},{1,2},{17,16},{2,3},{18,17},{3,0},{19,18},{32,33},{4... | collective-permute-start | bytes 2506760 | tf_op jit(solution)/shard_map/ppermute | solution.py:31
  21.9 0.1 shard_map.50
  22.0 0.6 collective-permute-start.9
  22.6 0.8 %collective-permute-start.13 = (bf16[544,768]{1,0:T(8,128)(2,1)S(1)}, bf16[544,768]{1,0:T(8,128)(2,1)S(1)}, u32[]{:S(2)}, u32[]{:S(2)}) collective-permute-start(bf16[544,768]{1,0:T(8,128)(2,1)S(1)} %collective-permute-done.2.refs_1_), channel_id=1, source_target_pairs={{0,96},{16,48},{1,97},{17,49},{2,98},{18,50},{3,99},{19,51},{32,0}... | collective-permute-start | bytes 2506760 | tf_op jit(solution)/shard_map/ppermute | solution.py:31
  23.5 0.1 collective-permute-start.11
  23.6 3.6 %shard_map.48.refs_10_ = f32[6,8,256]{2,1,0:T(8,128)S(1)} custom-call(bf16[544,768]{1,0:T(8,128)(2,1)S(1)} %shard_map.47.refs_0_, bf16[544,768]{1,0:T(8,128)(2,1)S(1)} %collective-permute-done.2.refs_1_, bf16[544,768]{1,0:T(8,128)(2,1)S(1)} %collective-permute-done.3.refs_2_, bf16[272,768]{1,0:T(8,128)(2,1)S(1)} %shard_map.46.own_ref.refs_3_.refs_7_, ...), custom_call_target="tpu_custom_call" | custom-call | flops 11796480 | bytes 10000 | tf_op jit(solution)/shard_map/pallas_call | solution.py:193
  27.1 8.0 %collective-permute-done.5.refs_0_.refs_3_ = bf16[544,768]{1,0:T(8,128)(2,1)S(1)} collective-permute-done((bf16[544,768]{1,0:T(8,128)(2,1)S(1)}, bf16[544,768]{1,0:T(8,128)(2,1)S(1)}, u32[]{:S(2)}, u32[]{:S(2)}) %collective-permute-start.5) | collective-permute-done | bytes 835616 | tf_op jit(solution)/shard_map/ppermute | solution.py:31
  35.1 3.4 %collective-permute-start.8 = (bf16[544,768]{1,0:T(8,128)(2,1)S(1)}, bf16[544,768]{1,0:T(8,128)(2,1)S(1)}, u32[]{:S(2)}, u32[]{:S(2)}) collective-permute-start(bf16[544,768]{1,0:T(8,128)(2,1)S(1)} %collective-permute-done.5.refs_0_.refs_3_), channel_id=1, source_target_pairs={{0,1},{16,19},{1,2},{17,16},{2,3},{18,17},{3,0},{19,18},{32,33},{4... | collective-permute-start | bytes 2506760 | tf_op jit(solution)/shard_map/ppermute | solution.py:31
  38.6 0.6 collective-permute-start.12
  39.2 0.8 %collective-permute-start.7 = (bf16[272,768]{1,0:T(8,128)(2,1)S(1)}, bf16[272,768]{1,0:T(8,128)(2,1)S(1)}, u32[]{:S(2)}, u32[]{:S(2)}) collective-permute-start(bf16[272,768]{1,0:T(8,128)(2,1)S(1)} %shard_map.49), channel_id=1, source_target_pairs={{0,12},{16,20},{1,13},{17,21},{2,14},{18,22},{3,15},{19,23},{32,44... | collective-permute-start | bytes 1253384 | tf_op jit(solution)/shard_map/ppermute | solution.py:31
  40.0 0.3 collective-permute-start.10
  40.3 6.7 %shard_map.53 = (f32[6,8,256]{2,1,0:T(8,128)S(1)}, f32[2,8,256]{2,1,0:T(8,128)S(1)}) custom-call(bf16[544,768]{1,0:T(8,128)(2,1)S(1)} %shard_map.47.refs_0_, bf16[544,768]{1,0:T(8,128)(2,1)S(1)} %collective-permute-done.2.refs_1_, bf16[544,768]{1,0:T(8,128)(2,1)S(1)} %collective-permute-done.3.refs_2_, ...), custom_call_target="tpu_custom_call" | custom-call | flops 22806528 | bytes 10000 | tf_op jit(solution)/shard_map/pallas_call | solution.py:193
  47.0 3.6 %collective-permute-done.12.refs_6_ = bf16[272,768]{1,0:T(8,128)(2,1)S(1)} collective-permute-done((bf16[272,768]{1,0:T(8,128)(2,1)S(1)}, bf16[272,768]{1,0:T(8,128)(2,1)S(1)}, u32[]{:S(2)}, u32[]{:S(2)}) %collective-permute-start.12) | collective-permute-done | bytes 417824 | tf_op jit(solution)/shard_map/ppermute | solution.py:31
  50.6 5.6 %collective-permute-done.7.refs_3_ = bf16[272,768]{1,0:T(8,128)(2,1)S(1)} collective-permute-done((bf16[272,768]{1,0:T(8,128)(2,1)S(1)}, bf16[272,768]{1,0:T(8,128)(2,1)S(1)}, u32[]{:S(2)}, u32[]{:S(2)}) %collective-permute-start.7) | collective-permute-done | bytes 417824 | tf_op jit(solution)/shard_map/ppermute | solution.py:31
  56.2 5.1 %shard_map.54 = f32[8,1,256]{2,1,0:T(1,128)S(1)} custom-call(bf16[544,768]{1,0:T(8,128)(2,1)S(1)} %shard_map.47.refs_0_, bf16[544,768]{1,0:T(8,128)(2,1)S(1)} %collective-permute-done.2.refs_1_, bf16[544,768]{1,0:T(8,128)(2,1)S(1)} %collective-permute-done.3.refs_2_, bf16[272,768]{1,0:T(8,128)(2,1)S(1)} %collective-permute-done.7.refs_3_, ...), custom_call_target="tpu_custom_call" | custom-call | flops 15728640 | bytes 10000 | tf_op jit(solution)/shard_map/pallas_call | solution.py:193
  61.4 9.1 %all_to_all.5 = f32[8,1,256]{2,1,0:T(1,128)S(1)} all-to-all(f32[8,1,256]{2,1,0:T(1,128)S(1)} %shard_map.54), channel_id=1, replica_groups=mesh['grp'=8,'blk'=16] {'grp'}, dimensions={0} | all-to-all | bytes 16384 | tf_op jit(solution)/shard_map/all_to_all | solution.py:264
  70.4 0.6 reduce_max.9
  (13 shorter events, 0.1 us)
Async XLA Ops:
  0.0 3.7 %collective-permute-start = (f32[256,768]{1,0:T(8,128)}, f32[256,768]{1,0:T(8,128)S(1)}, u32[]{:S(2)}, u32[]{:S(2)}) collective-permute-start(f32[256,768]{1,0:T(8,128)} %emb_ref.1), channel_id=1, source_target_pairs={{0,16},{16,0},{1,17},{17,1},{2,18},{18,2},{3,19},{19,3},{32,48},{4... | collective-permute-start | bytes 2359304 | tf_op jit(solution)/shard_map/ppermute | solution.py:31
  2.1 1.5 %collective-permute-start.1 = (s32[3,256]{1,0:T(4,128)S(1)}, s32[3,256]{1,0:T(4,128)S(1)}, u32[]{:S(2)}, u32[]{:S(2)}) collective-permute-start(s32[3,256]{1,0:T(4,128)S(1)} %pad_add_fusion.numbers_ref), channel_id=1, source_target_pairs={{0,16},{16,0},{1,17},{17,1},{2,18},{18,2},{3,19},{19,3},{32,48},{4... | collective-permute-start | bytes 9224 | tf_op jit(solution)/shard_map/ppermute | solution.py:31
  2.4 1.1 %copy-start = (f32[256,768]{1,0:T(8,128)S(1)}, f32[256,768]{1,0:T(8,128)}, u32[]{:S(2)}) copy-start(f32[256,768]{1,0:T(8,128)} %emb_ref.1) | copy-start | bytes 2359300
  3.8 12.8 %collective-permute-start.2 = (bf16[544,768]{1,0:T(8,128)(2,1)S(1)}, bf16[544,768]{1,0:T(8,128)(2,1)S(1)}, u32[]{:S(2)}, u32[]{:S(2)}) collective-permute-start(bf16[544,768]{1,0:T(8,128)(2,1)S(1)} %shard_map.47.refs_0_), channel_id=1, source_target_pairs={{0,96},{16,48},{1,97},{17,49},{2,98},{18,50},{3,99},{19,51},{32,0}... | collective-permute-start | bytes 2506760 | tf_op jit(solution)/shard_map/ppermute | solution.py:31
  5.3 12.6 %collective-permute-start.4 = (bf16[544,768]{1,0:T(8,128)(2,1)S(1)}, bf16[544,768]{1,0:T(8,128)(2,1)S(1)}, u32[]{:S(2)}, u32[]{:S(2)}) collective-permute-start(bf16[544,768]{1,0:T(8,128)(2,1)S(1)} %shard_map.47.refs_0_), channel_id=1, source_target_pairs={{0,12},{16,20},{1,13},{17,21},{2,14},{18,22},{3,15},{19,23},{32,44... | collective-permute-start | bytes 2506760 | tf_op jit(solution)/shard_map/ppermute | solution.py:31
  6.5 15.4 %collective-permute-start.6 = (bf16[544,768]{1,0:T(8,128)(2,1)S(1)}, bf16[544,768]{1,0:T(8,128)(2,1)S(1)}, u32[]{:S(2)}, u32[]{:S(2)}) collective-permute-start(bf16[544,768]{1,0:T(8,128)(2,1)S(1)} %shard_map.47.refs_0_), channel_id=1, source_target_pairs={{0,3},{16,17},{1,0},{17,18},{2,1},{18,19},{3,2},{19,16},{32,35},{4... | collective-permute-start | bytes 2506760 | tf_op jit(solution)/shard_map/ppermute | solution.py:31
  16.6 6.0 %collective-permute-start.3 = (bf16[544,768]{1,0:T(8,128)(2,1)S(1)}, bf16[544,768]{1,0:T(8,128)(2,1)S(1)}, u32[]{:S(2)}, u32[]{:S(2)}) collective-permute-start(bf16[544,768]{1,0:T(8,128)(2,1)S(1)} %collective-permute-done.2.refs_1_), channel_id=1, source_target_pairs={{0,16},{16,0},{1,17},{17,1},{2,18},{18,2},{3,19},{19,3},{32,48},{4... | collective-permute-start | bytes 2506760 | tf_op jit(solution)/shard_map/ppermute | solution.py:31
  17.8 17.3 %collective-permute-start.5 = (bf16[544,768]{1,0:T(8,128)(2,1)S(1)}, bf16[544,768]{1,0:T(8,128)(2,1)S(1)}, u32[]{:S(2)}, u32[]{:S(2)}) collective-permute-start(bf16[544,768]{1,0:T(8,128)(2,1)S(1)} %collective-permute-done.4.refs_4_.refs_0_.refs_8_), channel_id=1, source_target_pairs={{0,1},{16,19},{1,2},{17,16},{2,3},{18,17},{3,0},{19,18},{32,33},{4... | collective-permute-start | bytes 2506760 | tf_op jit(solution)/shard_map/ppermute | solution.py:31
  22.0 18.0 %collective-permute-start.9 = (bf16[816,768]{1,0:T(8,128)(2,1)S(1)}, bf16[816,768]{1,0:T(8,128)(2,1)S(1)}, u32[]{:S(2)}, u32[]{:S(2)}) collective-permute-start(bf16[816,768]{1,0:T(8,128)(2,1)S(1)} %shard_map.50), channel_id=1, source_target_pairs={{0,12},{16,20},{1,13},{17,21},{2,14},{18,22},{3,15},{19,23},{32,44... | collective-permute-start | bytes 3760136 | tf_op jit(solution)/shard_map/ppermute | solution.py:31
  22.6 17.6 %collective-permute-start.13 = (bf16[544,768]{1,0:T(8,128)(2,1)S(1)}, bf16[544,768]{1,0:T(8,128)(2,1)S(1)}, u32[]{:S(2)}, u32[]{:S(2)}) collective-permute-start(bf16[544,768]{1,0:T(8,128)(2,1)S(1)} %collective-permute-done.2.refs_1_), channel_id=1, source_target_pairs={{0,96},{16,48},{1,97},{17,49},{2,98},{18,50},{3,99},{19,51},{32,0}... | collective-permute-start | bytes 2506760 | tf_op jit(solution)/shard_map/ppermute | solution.py:31
  23.5 15.1 %collective-permute-start.11 = (bf16[272,768]{1,0:T(8,128)(2,1)S(1)}, bf16[272,768]{1,0:T(8,128)(2,1)S(1)}, u32[]{:S(2)}, u32[]{:S(2)}) collective-permute-start(bf16[272,768]{1,0:T(8,128)(2,1)S(1)} %shard_map.52), channel_id=1, source_target_pairs={{0,3},{16,17},{1,0},{17,18},{2,1},{18,19},{3,2},{19,16},{32,35},{4... | collective-permute-start | bytes 1253384 | tf_op jit(solution)/shard_map/ppermute | solution.py:31
  35.1 21.1 %collective-permute-start.8 = (bf16[544,768]{1,0:T(8,128)(2,1)S(1)}, bf16[544,768]{1,0:T(8,128)(2,1)S(1)}, u32[]{:S(2)}, u32[]{:S(2)}) collective-permute-start(bf16[544,768]{1,0:T(8,128)(2,1)S(1)} %collective-permute-done.5.refs_0_.refs_3_), channel_id=1, source_target_pairs={{0,1},{16,19},{1,2},{17,16},{2,3},{18,17},{3,0},{19,18},{32,33},{4... | collective-permute-start | bytes 2506760 | tf_op jit(solution)/shard_map/ppermute | solution.py:31
  38.6 12.0 %collective-permute-start.12 = (bf16[272,768]{1,0:T(8,128)(2,1)S(1)}, bf16[272,768]{1,0:T(8,128)(2,1)S(1)}, u32[]{:S(2)}, u32[]{:S(2)}) collective-permute-start(bf16[272,768]{1,0:T(8,128)(2,1)S(1)} %collective-permute-done.11.refs_5_), channel_id=1, source_target_pairs={{0,8},{16,24},{1,9},{17,25},{2,10},{18,26},{3,11},{19,27},{32,40},... | collective-permute-start | bytes 1253384 | tf_op jit(solution)/shard_map/ppermute | solution.py:31
  39.2 17.0 %collective-permute-start.7 = (bf16[272,768]{1,0:T(8,128)(2,1)S(1)}, bf16[272,768]{1,0:T(8,128)(2,1)S(1)}, u32[]{:S(2)}, u32[]{:S(2)}) collective-permute-start(bf16[272,768]{1,0:T(8,128)(2,1)S(1)} %shard_map.49), channel_id=1, source_target_pairs={{0,12},{16,20},{1,13},{17,21},{2,14},{18,22},{3,15},{19,23},{32,44... | collective-permute-start | bytes 1253384 | tf_op jit(solution)/shard_map/ppermute | solution.py:31
  40.0 16.2 %collective-permute-start.10 = (bf16[272,768]{1,0:T(8,128)(2,1)S(1)}, bf16[272,768]{1,0:T(8,128)(2,1)S(1)}, u32[]{:S(2)}, u32[]{:S(2)}) collective-permute-start(bf16[272,768]{1,0:T(8,128)(2,1)S(1)} %shard_map.51), channel_id=1, source_target_pairs={{0,3},{16,17},{1,0},{17,18},{2,1},{18,19},{3,2},{19,16},{32,35},{4... | collective-permute-start | bytes 1253384 | tf_op jit(solution)/shard_map/ppermute | solution.py:31
